TPU v7x, 256 devices: a whole 4x4x8 slice. The times are simulated.
256 devices in a mesh: tm: 8 (over x, core), tile: 32 (over y, z).
Axes of the slice: x: 4, y: 4, z: 8, core: 2. Of those that a mesh axis runs over, the one named last changes fastest.
Arguments:
- features: bfloat16 [48, 96, 24, 512], P('tm', 'tile')
- frame_counts: int32 [8], P('tm'), may hold values from 2 to 6, as said below
- row_lengths: int32 [32], P('tile'), may hold values from 1 to 3, 64 in all
- norm_gain: float32 [512], replicated, may hold values from 0.5 to 2
- norm_shift: float32 [512], replicated, may hold values from -3 to 3
- conv_weight: bfloat16 [3, 3, 3, 512, 256], replicated, may hold values from -0.0546875 to 0.0546875
- conv_bias: float32 [256], replicated, may hold values from -3 to 3
Outputs:
- upscaled: bfloat16 [48, 192, 48, 256], P('tm', 'tile')
Inputs may be any that keep to these rules, and one draw needn't show every extreme that they name: `frame_counts`: live frames are the first frame slots of each time block; some block is full. `row_lengths`: live latent rows are the first row slots of each tile; some tile is full.
All inputs are finite; a program needn't handle non-finite values. No bound on the sum of `row_lengths` on one device may be relied on, other than what follows from the above.
Results may differ from a plain program's by a relative error of at most 0.0046.
Values may be sent and summed in bfloat16 or wider, within the bound.
A program may use at most 128 MiB of HBM per device.

v0:
```python
import jax
import jax.numpy as jnp
from jax import lax
from jax.sharding import PartitionSpec as P

GROUPS = 32


EPSILON = 1e-06


def passed_along(value, axis, steps):
    count = lax.axis_size(axis)
    leading, last = (max(0, -steps), min(count, count - steps))
    return lax.ppermute(value, axis, [(source, source + steps) for source in range(leading, last)])


def upscale(block):
    return jnp.repeat(jnp.repeat(block, 2, axis=1), 2, axis=2)


def take_prior(block):
    return passed_along(block, "tm", 1)


def from_above(block):
    return passed_along(block, "tile", 1)


def from_below(block):
    return passed_along(block, "tile", -1)


def extend_time(block, count_here):
    recent = lax.dynamic_slice_in_dim(block, count_here - 2, 2, 0)
    arrived = take_prior(recent)
    opening = jnp.concatenate([block[:1], block[:1]], 0)
    prior = jnp.where(lax.axis_index("tm") == 0, opening, arrived)
    return jnp.concatenate([prior, block], 0)


def extend_rows(block, last_row):
    closing = lax.dynamic_slice_in_dim(block, last_row, 1, 1)
    upper = from_above(closing)
    lower = from_below(block[:, :1])
    blank = jnp.zeros_like(upper)
    stacked = jnp.concatenate([upper, block, blank], 1)
    position = lax.broadcasted_iota(jnp.int32, (1, stacked.shape[1], 1, 1), 1)
    return jnp.where(position == last_row + 2, lower, stacked)


def body(features, frame_counts, row_lengths, norm_gain, norm_shift, conv_weight, conv_bias):
    frames, height, width, channels = features.shape
    count_here = frame_counts[0]
    length_here = row_lengths[0]
    span = channels // GROUPS
    frame_live = (jnp.arange(frames) < count_here).astype(jnp.float32)
    row_live = (jnp.arange(height) < length_here).astype(jnp.float32)
    mask = frame_live[:, None] * row_live[None, :]
    values = features.astype(jnp.float32).reshape(frames, height, width, GROUPS, span)
    weight_mask = mask[:, :, None, None, None]
    local_cells = jnp.sum(mask) * (width * span)
    local_sums = jnp.sum(values * weight_mask, axis=(0, 1, 2, 4))
    totals, cells = lax.psum((local_sums, local_cells), ("tm", "tile"))
    mean = totals / cells
    centered = values - mean[:, None]
    local_spread = jnp.sum(centered * centered * weight_mask, axis=(0, 1, 2, 4))
    variance = lax.psum(local_spread, ("tm", "tile")) / cells
    scale = lax.rsqrt(variance + EPSILON)
    normed = ((values - mean[:, None]) * scale[:, None]).reshape(frames, height, width, channels)
    hidden = jax.nn.silu(normed * norm_gain + norm_shift).astype(jnp.bfloat16)
    widened = extend_rows(extend_time(upscale(hidden), count_here), 2 * length_here - 1)
    widened = jnp.pad(widened, ((0, 0), (0, 0), (1, 1), (0, 0)))
    fine_height = 2 * height
    fine_width = 2 * width
    total = jnp.zeros((frames, fine_height, fine_width, conv_weight.shape[-1]), jnp.float32)
    for vertical in range(3):
        for horizontal in range(3):
            window = widened[
                :, vertical : vertical + fine_height, horizontal : horizontal + fine_width
            ]
            stacked = jnp.concatenate(
                [window[0:frames], window[1 : frames + 1], window[2 : frames + 2]], axis=-1
            )
            kernel = conv_weight[:, vertical, horizontal].reshape(3 * channels, -1)
            total = total + jnp.einsum(
                "fhwc,cd->fhwd", stacked, kernel, preferred_element_type=jnp.float32
            )
    fine_live = (jnp.arange(fine_height) < 2 * length_here).astype(jnp.float32)
    upscaled = (
        (total + conv_bias) * frame_live[:, None, None, None] * fine_live[None, :, None, None]
    )
    return upscaled.astype(jnp.bfloat16)


def solution(mesh):
    in_specs = (P("tm", "tile", None, None), P("tm"), P("tile"), P(), P(), P(), P())
    out_specs = P("tm", "tile", None, None)
    return jax.shard_map(body, mesh=mesh, in_specs=in_specs, out_specs=out_specs, check_vma=False)
```

profile of v0, /device:TPU:12, one launch (start us, length us, event | category | flops | bytes accessed | tf_op | source)
XLA Modules:
  0.0 242.1 jit_solution(10319614832710314723)
XLA Ops:
  1.3 0.7 fusion.71
  2.0 1.2 fusion.68
  3.2 0.1 reduce_sum.32
  3.9 0.1 reduce_sum.36
  4.0 77.1 %all-reduce.1 = (f32[32]{0:T(128)S(1)}, f32[]{:T(128)}) all-reduce(f32[32]{0:T(128)S(1)} %reduce_sum.36, f32[]{:T(128)S(6)} %mul.91), channel_id=1, replica_groups=mesh['tm'=8,'tile'=32] {'tm','tile'}, use_global_device_ids=true, to_apply=%region_2.0 | all-reduce | flops 33 | bytes 264 | tf_op jit(solution)/shard_map/psum | solution.py:64
  81.1 0.6 broadcast_divide_fusion
  81.8 0.1 sub.25
  81.9 1.2 fusion.59
  83.1 0.1 reduce_sum.46
  83.2 0.1 reduce_sum.47
  83.3 73.7 %psum.23 = f32[32]{0:T(128)S(1)} all-reduce(f32[32]{0:T(128)S(1)} %reduce_sum.47), channel_id=1, replica_groups=mesh['tm'=8,'tile'=32] {'tm','tile'}, use_global_device_ids=true, to_apply=%region_7.8 | all-reduce | flops 32 | bytes 256 | tf_op jit(solution)/shard_map/psum | solution.py:68
  157.1 0.7 add_rsqrt_fusion
  157.8 0.1 mul.95
  157.9 1.4 fusion.67
  159.3 0.7 copy-done
  160.0 1.6 broadcast_in_dim.49
  161.6 0.7 reshape.80
  162.4 1.9 collective-permute-start
  164.3 0.9 slice_bitcast_fusion
  165.2 0.2 broadcast_in_dim.46
  165.4 0.1 broadcast_in_dim.47
  165.6 8.0 %collective-permute-done = bf16[2,6,48,512]{3,2,1,0:T(8,128)(2,1)S(1)} collective-permute-done((bf16[2,6,48,512]{3,2,1,0:T(8,128)(2,1)S(1)}, bf16[2,6,48,512]{3,2,1,0:T(8,128)(2,1)S(1)}, u32[]{:S(2)}, u32[]{:S(2)}) %collective-permute-start) | collective-permute-done | bytes 589856 | tf_op jit(solution)/shard_map/ppermute | solution.py:15
  173.8 4.5 %collective-permute-start.1 = (bf16[8,1,48,512]{3,2,1,0:T(8,128)(2,1)S(1)}, bf16[8,1,48,512]{3,2,1,0:T(8,128)(2,1)S(1)}, u32[]{:S(2)}, u32[]{:S(2)}) collective-permute-start(bf16[8,1,48,512]{3,2,1,0:T(8,128)(2,1)S(1)} %get-tuple-element.43), channel_id=1, source_target_pairs={{1,0},{2,1},{3,2},{4,3},{5,4},{6,5},{7,6},{8,7},{9,8},{10,9},{11,1... | collective-permute-start | bytes 1179656 | tf_op jit(solution)/shard_map/ppermute | solution.py:15
  178.2 2.1 collective-permute-start.2
  180.4 6.0 %fusion.81 = (bf16[3,1,1,512,256]{4,3,2,1,0:T(8,128)(2,1)}, bf16[3,1,1,512,256]{4,3,2,1,0:T(8,128)(2,1)}, bf16[3,1,1,512,256]{4,3,2,1,0:T(8,128)(2,1)}, bf16[3,1...) fusion(bf16[3,3,3,512,256]{4,3,2,1,0:T(8,128)(2,1)} %param.12), kind=kLoop, calls=%fused_computation.115 | loop fusion | bytes 14155776 | tf_op jit(solution)/shard_map/slice | solution.py:85
  186.4 6.1 %collective-permute-done.2 = bf16[8,1,48,512]{3,2,1,0:T(8,128)(2,1)S(1)} collective-permute-done((bf16[8,1,48,512]{3,2,1,0:T(8,128)(2,1)S(1)}, bf16[8,1,48,512]{3,2,1,0:T(8,128)(2,1)S(1)}, u32[]{:S(2)}, u32[]{:S(2)}) %collective-permute-start.2) | collective-permute-done | bytes 393248 | tf_op jit(solution)/shard_map/ppermute | solution.py:15
  192.5 0.5 maximum_select_fusion
  193.0 2.0 fusion.82
  195.0 21.5 %pad_slice_fusion.4 = (bf16[6,6,48,512]{3,2,1,0:T(8,128)(2,1)S(1)}, bf16[6,6,48,512]{3,2,1,0:T(8,128)(2,1)}, bf16[6,6,48,512]{3,2,1,0:T(8,128)(2,1)}, bf16[6,6,4...) fusion(bf16[8,8,48,512]{3,2,1,0:T(8,128)(2,1)S(1)} %maximum_sel, ...), kind=kLoop, calls=%fused_computation.77 | loop fusion | bytes 40304640 | tf_op jit(solution)/shard_map/slice | solution.py:83
  216.5 2.8 %fusion.6 = f32[6,6,48,256]{3,2,1,0:T(8,128)S(1)} fusion(bf16[1536,256,1,1]{1,0,3,2:T(8,128)(2,1)} %bitcast.76, bf16[6,6,48,512]{3,2,1,0:T(8,128)(2,1)S(1)} %get-tuple-element.40, bf16[6,6,48,512]{3,2,1,0:T(8,128)(2,1)S(1)} %get-tuple-element.41, bf16[6,6,48,512]{3,2,1,0:T(8,128)(2,1)S(1)} %get-tuple-element.35), kind=kOutput, calls=%fused_computation.6 | convolution fusion | flops 1374879744 | bytes 7864320 | tf_op jit(solution)/shard_map/fhwc,cd->fhwd/dot_general | solution.py:86
  219.3 2.7 %fusion.24 = f32[6,6,48,256]{3,2,1,0:T(8,128)} fusion(bf16[1536,256,1,1]{1,0,3,2:T(8,128)(2,1)S(1)} %bitcast.75, bf16[6,6,48,512]{3,2,1,0:T(8,128)(2,1)S(1)} %get-tuple-element.37, bf16[6,6,48,512]{3,2,1,0:T(8,128)(2,1)S(1)} %get-tuple-element.38, bf16[6,6,48,512]{3,2,1,0:T(8,128)(2,1)S(1)} %get-tuple-element.39), kind=kOutput, calls=%fused_computation.24 | convolution fusion | flops 1374879744 | bytes 7864320 | tf_op jit(solution)/shard_map/fhwc,cd->fhwd/dot_general | solution.py:86
  222.1 2.7 %fusion.42 = f32[6,6,48,256]{3,2,1,0:T(8,128)} fusion(bf16[1536,256,1,1]{1,0,3,2:T(8,128)(2,1)S(1)} %bitcast.74, bf16[6,6,48,512]{3,2,1,0:T(8,128)(2,1)S(1)} %copy-done.17, bf16[6,6,48,512]{3,2,1,0:T(8,128)(2,1)S(1)} %copy-done.18, bf16[6,6,48,512]{3,2,1,0:T(8,128)(2,1)S(1)} %get-tuple-element.36), kind=kOutput, calls=%fused_computation.42 | convolution fusion | flops 1374879744 | bytes 7864320 | tf_op jit(solution)/shard_map/fhwc,cd->fhwd/dot_general | solution.py:86
  224.8 2.1 fusion
  226.9 0.4 copy-done.14
  227.3 0.2 copy-done.23
  227.5 2.1 fusion.12
  229.6 0.4 copy-done.11
  230.0 0.2 copy-done.22
  230.2 2.1 fusion.18
  232.3 0.4 copy-done.8
  232.7 0.2 copy-done.21
  232.9 2.1 fusion.30
  235.0 0.4 copy-done.5
  235.4 0.2 copy-done.20
  235.6 2.1 fusion.36
  237.8 0.6 copy-done.28
  238.4 0.5 copy-done.29
  238.9 3.1 %multiply_convert_fusion = bf16[6,6,48,256]{3,2,1,0:T(8,128)(2,1)} fusion(f32[6,6,48,256]{3,2,1,0:T(8,128)S(1)} %copy-done.29, f32[6,6,48,256]{3,2,1,0:T(8,128)S(1)} %fusion.36, f32[6,6,48,256]{3,2,1,0:T(8,128)S(1)} %fusion.30, f32[6,6,48,256]{3,2,1,0:T(8,128)S(1)} %copy-done.28, f32[6,6,48,256]{3,2,1,0:T(8,128)S(1)} %fusion.18, ...), kind=kOutput, calls=%fused_computation.59 | convolution fusion | flops 1380188160 | bytes 21136432 | tf_op jit(solution)/shard_map/fhwc,cd->fhwd/dot_general | solution.py:86
  (62 shorter events, 0.7 us)
Async XLA Ops:
  159.2 0.8 copy-start
  162.4 11.2 %collective-permute-start = (bf16[2,6,48,512]{3,2,1,0:T(8,128)(2,1)S(1)}, bf16[2,6,48,512]{3,2,1,0:T(8,128)(2,1)S(1)}, u32[]{:S(2)}, u32[]{:S(2)}) collective-permute-start(bf16[2,6,48,512]{3,2,1,0:T(8,128)(2,1)S(1)} %constant_dynamic-slice_fusion), channel_id=1, source_target_pairs={{0,32},{32,64},{64,96},{96,128},{128,160},{160,192},{192,224},{1,3... | collective-permute-start | bytes 1769480 | tf_op jit(solution)/shard_map/ppermute | solution.py:15
  173.8 12.6 %collective-permute-start.1 = (bf16[8,1,48,512]{3,2,1,0:T(8,128)(2,1)S(1)}, bf16[8,1,48,512]{3,2,1,0:T(8,128)(2,1)S(1)}, u32[]{:S(2)}, u32[]{:S(2)}) collective-permute-start(bf16[8,1,48,512]{3,2,1,0:T(8,128)(2,1)S(1)} %get-tuple-element.43), channel_id=1, source_target_pairs={{1,0},{2,1},{3,2},{4,3},{5,4},{6,5},{7,6},{8,7},{9,8},{10,9},{11,1... | collective-permute-start | bytes 1179656 | tf_op jit(solution)/shard_map/ppermute | solution.py:15
  178.2 14.2 %collective-permute-start.2 = (bf16[8,1,48,512]{3,2,1,0:T(8,128)(2,1)S(1)}, bf16[8,1,48,512]{3,2,1,0:T(8,128)(2,1)S(1)}, u32[]{:S(2)}, u32[]{:S(2)}) collective-permute-start(bf16[8,1,48,512]{3,2,1,0:T(8,128)(2,1)S(1)} %get-tuple-element.44), channel_id=1, source_target_pairs={{0,1},{1,2},{2,3},{3,4},{4,5},{5,6},{6,7},{7,8},{8,9},{9,10},{10,1... | collective-permute-start | bytes 1179656 | tf_op jit(solution)/shard_map/ppermute | solution.py:15
  216.5 2.8 %copy-start.26 = (bf16[3,1,1,512,256]{4,3,2,1,0:T(8,128)(2,1)S(1)}, bf16[3,1,1,512,256]{4,3,2,1,0:T(8,128)(2,1)}, u32[]{:S(2)}) copy-start(bf16[3,1,1,512,256]{4,3,2,1,0:T(8,128)(2,1)} %get-tuple-element.10) | copy-start | bytes 2359300
  219.3 2.7 %copy-start.17 = (bf16[6,6,48,512]{3,2,1,0:T(8,128)(2,1)S(1)}, bf16[6,6,48,512]{3,2,1,0:T(8,128)(2,1)}, u32[]{:S(2)}) copy-start(bf16[6,6,48,512]{3,2,1,0:T(8,128)(2,1)} %get-tuple-element.33) | copy-start | bytes 5308420
  219.3 2.7 %copy-start.18 = (bf16[6,6,48,512]{3,2,1,0:T(8,128)(2,1)S(1)}, bf16[6,6,48,512]{3,2,1,0:T(8,128)(2,1)}, u32[]{:S(2)}) copy-start(bf16[6,6,48,512]{3,2,1,0:T(8,128)(2,1)} %get-tuple-element.34) | copy-start | bytes 5308420
  219.3 2.7 %copy-start.25 = (bf16[3,1,1,512,256]{4,3,2,1,0:T(8,128)(2,1)S(1)}, bf16[3,1,1,512,256]{4,3,2,1,0:T(8,128)(2,1)}, u32[]{:S(2)}) copy-start(bf16[3,1,1,512,256]{4,3,2,1,0:T(8,128)(2,1)} %get-tuple-element.15) | copy-start | bytes 2359300
  222.0 2.7 %copy-start.15 = (bf16[6,6,48,512]{3,2,1,0:T(8,128)(2,1)S(1)}, bf16[6,6,48,512]{3,2,1,0:T(8,128)(2,1)}, u32[]{:S(2)}) copy-start(bf16[6,6,48,512]{3,2,1,0:T(8,128)(2,1)} %get-tuple-element.17) | copy-start | bytes 5308420
  222.0 2.7 %copy-start.16 = (bf16[6,6,48,512]{3,2,1,0:T(8,128)(2,1)S(1)}, bf16[6,6,48,512]{3,2,1,0:T(8,128)(2,1)}, u32[]{:S(2)}) copy-start(bf16[6,6,48,512]{3,2,1,0:T(8,128)(2,1)} %get-tuple-element.18) | copy-start | bytes 5308420
  222.0 2.7 %copy-start.24 = (bf16[3,1,1,512,256]{4,3,2,1,0:T(8,128)(2,1)S(1)}, bf16[3,1,1,512,256]{4,3,2,1,0:T(8,128)(2,1)}, u32[]{:S(2)}) copy-start(bf16[3,1,1,512,256]{4,3,2,1,0:T(8,128)(2,1)} %get-tuple-element.14) | copy-start | bytes 2359300
  224.7 2.1 copy-start.12
  224.7 2.1 copy-start.13
  224.7 2.5 %copy-start.14 = (bf16[6,6,48,512]{3,2,1,0:T(8,128)(2,1)S(1)}, bf16[6,6,48,512]{3,2,1,0:T(8,128)(2,1)}, u32[]{:S(2)}) copy-start(bf16[6,6,48,512]{3,2,1,0:T(8,128)(2,1)} %get-tuple-element.21) | copy-start | bytes 5308420
  224.8 2.7 %copy-start.23 = (bf16[3,1,1,512,256]{4,3,2,1,0:T(8,128)(2,1)S(1)}, bf16[3,1,1,512,256]{4,3,2,1,0:T(8,128)(2,1)}, u32[]{:S(2)}) copy-start(bf16[3,1,1,512,256]{4,3,2,1,0:T(8,128)(2,1)} %get-tuple-element.12) | copy-start | bytes 2359300
  227.4 2.1 copy-start.9
  227.4 2.1 copy-start.10
  227.4 2.5 %copy-start.11 = (bf16[6,6,48,512]{3,2,1,0:T(8,128)(2,1)S(1)}, bf16[6,6,48,512]{3,2,1,0:T(8,128)(2,1)}, u32[]{:S(2)}) copy-start(bf16[6,6,48,512]{3,2,1,0:T(8,128)(2,1)} %get-tuple-element.24) | copy-start | bytes 5308420
  227.4 2.7 %copy-start.22 = (bf16[3,1,1,512,256]{4,3,2,1,0:T(8,128)(2,1)S(1)}, bf16[3,1,1,512,256]{4,3,2,1,0:T(8,128)(2,1)}, u32[]{:S(2)}) copy-start(bf16[3,1,1,512,256]{4,3,2,1,0:T(8,128)(2,1)} %get-tuple-element.11) | copy-start | bytes 2359300
  230.2 2.1 copy-start.6
  230.2 2.1 copy-start.7
  230.2 2.5 %copy-start.8 = (bf16[6,6,48,512]{3,2,1,0:T(8,128)(2,1)S(1)}, bf16[6,6,48,512]{3,2,1,0:T(8,128)(2,1)}, u32[]{:S(2)}) copy-start(bf16[6,6,48,512]{3,2,1,0:T(8,128)(2,1)} %get-tuple-element.27) | copy-start | bytes 5308420
  230.2 2.7 %copy-start.21 = (bf16[3,1,1,512,256]{4,3,2,1,0:T(8,128)(2,1)S(1)}, bf16[3,1,1,512,256]{4,3,2,1,0:T(8,128)(2,1)}, u32[]{:S(2)}) copy-start(bf16[3,1,1,512,256]{4,3,2,1,0:T(8,128)(2,1)} %get-tuple-element.9) | copy-start | bytes 2359300
  232.9 2.1 copy-start.3
  232.9 2.1 copy-start.4
  232.9 2.5 %copy-start.5 = (bf16[6,6,48,512]{3,2,1,0:T(8,128)(2,1)S(1)}, bf16[6,6,48,512]{3,2,1,0:T(8,128)(2,1)}, u32[]{:S(2)}) copy-start(bf16[6,6,48,512]{3,2,1,0:T(8,128)(2,1)} %get-tuple-element.30) | copy-start | bytes 5308420
  232.9 2.7 %copy-start.20 = (bf16[3,1,1,512,256]{4,3,2,1,0:T(8,128)(2,1)S(1)}, bf16[3,1,1,512,256]{4,3,2,1,0:T(8,128)(2,1)}, u32[]{:S(2)}) copy-start(bf16[3,1,1,512,256]{4,3,2,1,0:T(8,128)(2,1)} %get-tuple-element.8) | copy-start | bytes 2359300
  235.6 2.1 copy-start.1
  235.6 2.1 copy-start.2
  235.6 2.2 copy-start.19
  235.6 2.2 copy-start.27
  235.6 2.8 %copy-start.28 = (f32[6,6,48,256]{3,2,1,0:T(8,128)S(1)}, f32[6,6,48,256]{3,2,1,0:T(8,128)}, u32[]{:S(2)}) copy-start(f32[6,6,48,256]{3,2,1,0:T(8,128)} %fusion.24) | copy-start | bytes 5308420
  235.6 3.3 %copy-start.29 = (f32[6,6,48,256]{3,2,1,0:T(8,128)S(1)}, f32[6,6,48,256]{3,2,1,0:T(8,128)}, u32[]{:S(2)}) copy-start(f32[6,6,48,256]{3,2,1,0:T(8,128)} %fusion.42) | copy-start | bytes 5308420
where the time goes:
time: 243 us; the launch traced here: 242 us
  blocking collectives  151 us (62%)
  local copies, waits for them, and re-layouts  37.9 us (16%)
  matrix products  21.6 us (9%)
  waiting for transfers between devices  14.1 us (6%)
  starting transfers between devices  8.5 us (3%)
  other arithmetic  6.63 us (3%)
    psum x1, blocking collectives, body(): totals, cells = lax.psum((local_sums, local_cells), ('tm', 'tile'))  77.1 us
    psum x1, blocking collectives, body(): variance = lax.psum(local_spread, ('tm', 'tile')) / cells  73.7 us
    slice x2, local copies, waits for them, and re-layouts, body(): window[0:frames]  23.5 us
    dot_general x9, matrix products, body(): jnp.einsum('fhwc,cd->fhwd', stacked, kernel, preferred_element_type=jnp.f...  21.6 us
    ppermute x3, waiting for transfers between devices, passed_along(): lax.ppermute(value, axis, [(source, source + steps) for source in range(l...  14.1 us
    ppermute x3, starting transfers between devices, passed_along(): lax.ppermute(value, axis, [(source, source + steps) for source in range(l...  8.5 us
    slice x1, local copies, waits for them, and re-layouts, body(): kernel = conv_weight[:, vertical, horizontal].reshape(3 * channels, -1)  6 us
  transfers between devices with their start and end apart: 3, of which 2 were waited for; matrix products, arithmetic and copies ran while one was open for 3% of the time, Pallas kernels for 0%

commit v1 on v0

v1 whole, which is shorter than its diff:
```python
import functools

import jax
import jax.numpy as jnp
from jax import lax
from jax.experimental import pallas as pl
from jax.experimental.pallas import tpu as pltpu
from jax.sharding import PartitionSpec as P

GROUPS = 32
EPSILON = 1e-06
MESH = pl.DeviceIdType.MESH
LANES = 128
VMEM_LIMIT = 56 * 1024 * 1024


def group_matrix(channels, offset, transposed):
    span = channels // GROUPS
    shape = (LANES, channels) if transposed else (channels, LANES)
    channel = lax.broadcasted_iota(jnp.int32, shape, 1 if transposed else 0)
    lane = lax.broadcasted_iota(jnp.int32, shape, 0 if transposed else 1)
    low = (lane - offset) * span
    return ((channel >= low) & (channel < low + span)).astype(jnp.float32)


def exact_dot(a, b):
    return jnp.dot(a, b, precision=lax.Precision.HIGHEST, preferred_element_type=jnp.float32)


def merge(rows):
    totals = functools.reduce(lambda a, b: a + b, rows)
    counts = [pltpu.roll(row, LANES - 2 * GROUPS, 1) for row in rows]
    entries = pltpu.roll(totals, LANES - 2 * GROUPS, 1)
    mean = totals / entries
    between = jnp.zeros_like(totals)
    for row, count in zip(rows, counts):
        off = row / count - mean
        between = between + count * (off * off)
    spread = pltpu.roll(totals, LANES - GROUPS, 1) + between
    return totals, spread, entries


def as_row(totals, spread, entries):
    lane = lax.broadcasted_iota(jnp.int32, totals.shape, 1)
    spread = pltpu.roll(spread, GROUPS, 1)
    entries = pltpu.roll(entries, 2 * GROUPS, 1)
    row = jnp.where(lane < GROUPS, totals, jnp.where(lane < 2 * GROUPS, spread, entries))
    return jnp.where(lane < 3 * GROUPS, row, 1.0)


def exchange_kernel(
    dims, features, counts_in, lengths_in,
    stats, prior, upper, lower,
    block, tail, rising, sinking, first, second, counts, lengths,
    local_sems, send_sem, first_sem, second_sem, halo_sems,
):
    size_x, size_y, size_z, n_tm, n_tile = dims
    frames, height, width, channels = block.shape
    tm, tile = lax.axis_index("tm"), lax.axis_index("tile")
    x, core = tm // 2, tm % 2
    y, z = tile // size_z, tile % size_z

    def near(dz, dc):
        return (x * 2 + (core + dc) % 2, y * size_z + (z + dz) % size_z)

    def far(dx, dy):
        return (((x + dx) % size_x) * 2 + core, ((y + dy) % size_y) * size_z + z)

    def beside(dt, dr):
        return ((tm + dt + n_tm) % n_tm, (tile + dr + n_tile) % n_tile)

    near_steps = [(dz, dc) for dz in range(size_z) for dc in range(2)][1:]
    far_steps = [(dx, dy) for dx in range(size_x) for dy in range(size_y)][1:]
    halo_steps = [(a, b) for a in (-1, 0, 1) for b in (-1, 0, 1) if (a, b) != (0, 0)]

    load = pltpu.make_async_copy(features, block, local_sems.at[0])
    load.start()
    load_counts = pltpu.make_async_copy(counts_in, counts, local_sems.at[1])
    load_counts.start()
    load_lengths = pltpu.make_async_copy(lengths_in, lengths, local_sems.at[2])
    load_lengths.start()

    barrier = pltpu.get_barrier_semaphore()
    partners = [near(*s) for s in near_steps] + [far(*s) for s in far_steps]
    partners = partners + [beside(*s) for s in halo_steps]
    for partner in partners:
        pl.semaphore_signal(barrier, inc=1, device_id=partner, device_id_type=MESH)

    load_counts.wait()
    load_lengths.wait()
    load.wait()
    count_here = counts[0]
    length_here = lengths[0]

    recent = jnp.maximum(count_here - 2, 0)
    last_row = jnp.maximum(length_here - 1, 0)
    for k in range(2):
        tail[k] = block[recent + k]
        rising[k] = tail[k, last_row]
        sinking[k] = tail[k, 0]
    for k in range(frames):
        rising[2 + k] = block[k, last_row]
        sinking[2 + k] = block[k, 0]

    cells = (count_here * length_here * (width * (channels // GROUPS))).astype(jnp.float32)
    spread_out = group_matrix(channels, 0, True)
    gather = group_matrix(channels, 0, False)

    def over_live(term):
        total = jnp.zeros((8, channels), jnp.float32)
        for f in range(frames):
            for r in range(height):
                live = (f < count_here) & (r < length_here)
                part = term(block[f, r].astype(jnp.float32))
                part = jnp.where(live, part, 0.0)
                total = total + sum(part[8 * i : 8 * i + 8] for i in range(width // 8))
        return jnp.sum(exact_dot(total, gather), axis=0, keepdims=True)

    sums = over_live(lambda v: v)
    centre = exact_dot(jnp.broadcast_to(sums / cells, (8, LANES)), spread_out)[:1]
    spread = over_live(lambda v: (v - centre) * (v - centre))
    entries = jnp.zeros_like(sums) + cells
    first[0] = as_row(sums, spread, entries)

    pl.semaphore_wait(barrier, len(partners))

    copies = []

    def send(source, target, sem, device):
        copy = pltpu.make_async_remote_copy(
            src_ref=source, dst_ref=target, send_sem=send_sem, recv_sem=sem,
            device_id=device, device_id_type=MESH,
        )
        copy.start()
        return copy

    for i, step in enumerate(near_steps):
        send(first.at[0], first.at[1 + i], first_sem, near(*step))
    halos = [
        send(rising.at[pl.ds(2, frames)], upper.at[pl.ds(2, frames)], halo_sems.at[0], beside(0, 1)),
        send(sinking.at[pl.ds(2, frames)], lower.at[pl.ds(2, frames)], halo_sems.at[1], beside(0, -1)),
        send(rising.at[pl.ds(0, 2)], upper.at[pl.ds(0, 2)], halo_sems.at[2], beside(1, 1)),
        send(sinking.at[pl.ds(0, 2)], lower.at[pl.ds(0, 2)], halo_sems.at[3], beside(1, -1)),
        send(tail, prior, halo_sems.at[4], beside(1, 0)),
    ]

    arrived = first.at[pl.ds(1, len(near_steps))]
    pltpu.make_async_copy(arrived, arrived, first_sem).wait()
    second[0] = as_row(*merge([first[i] for i in range(1 + len(near_steps))]))
    for i, step in enumerate(far_steps):
        send(second.at[0], second.at[1 + i], second_sem, far(*step))
    arrived = second.at[pl.ds(1, len(far_steps))]
    pltpu.make_async_copy(arrived, arrived, second_sem).wait()
    totals, spread, entries = merge([second[i] for i in range(1 + len(far_steps))])
    mean = totals / entries
    scale = lax.rsqrt(spread / entries + EPSILON)
    both = jnp.concatenate([mean, scale, jnp.zeros((6, LANES), jnp.float32)], 0)
    lane = lax.broadcasted_iota(jnp.int32, both.shape, 1)
    stats[...] = exact_dot(jnp.where(lane < GROUPS, both, 0.0), spread_out)

    for halo in halos:
        halo.wait_recv()
    sent = first.at[pl.ds(1, len(near_steps))]
    pltpu.make_async_copy(sent, sent, send_sem).wait()
    sent = second.at[pl.ds(1, len(far_steps))]
    pltpu.make_async_copy(sent, sent, send_sem).wait()
    for halo in halos:
        halo.wait_send()


def convolve_kernel(
    n_tile, features, prior, upper, lower, weights, stats, gain, shift, bias, counts, lengths,
    out,
    raw, hidden, stacked, held, q0, q1, q2, rows, woven,
    raw_sem, weight_sems,
):
    frames, height, width, channels = features.shape
    slots = height + 2
    run = frames * width
    tm, tile = lax.axis_index("tm"), lax.axis_index("tile")
    count_here = counts[0]
    length_here = lengths[0]

    loads = []
    for r in range(height):
        loads.append((features.at[:, r], raw.at[1 + r, pl.ds(2, frames)]))
        loads.append((prior.at[:, r], raw.at[1 + r, pl.ds(0, 2)]))
    loads.append((upper, raw.at[0]))
    loads.append((lower, raw.at[slots - 1]))
    loads = [pltpu.make_async_copy(a, b, raw_sem.at[i]) for i, (a, b) in enumerate(loads)]
    for load in loads:
        load.start()
    order = [(v, h) for h in range(3) for v in range(3)]
    fetches = {}
    for v, h in order:
        i = v * 3 + h
        fetches[v, h] = pltpu.make_async_copy(weights.at[:, v, h], held.at[i], weight_sems.at[i])
        fetches[v, h].start()
    for load in loads:
        load.wait()

    mean = stats[0:1]
    scale = stats[1:2] * gain[...]
    offset = shift[...]
    for slot in range(slots):
        is_lower = slot == length_here + 1
        source = jnp.where(is_lower, slots - 1, slot)
        blank = (slot == 0) & (tile == 0) | is_lower & (tile == n_tile - 1)
        for k in range(frames + 2):
            frame = jnp.where(tm == 0, 2, k) if k < 2 else k
            v = raw[source, frame].astype(jnp.float32)
            v = (v - mean) * scale + offset
            v = v / (1.0 + jnp.exp(-v))
            hidden[pl.ds(k * width, width)] = jnp.where(blank, 0.0, v)
        for a in range(3):
            stacked[pl.ds(slot * run, run), pl.ds(a * channels, channels)] = hidden[
                pl.ds(a * width, run)
            ].astype(jnp.bfloat16)

    pad = 8
    for h in range(3):
        for v, q in enumerate((q0, q1, q2)):
            fetches[v, h].wait()
            depth = 3 * channels
            kernel = held[v * 3 + h].reshape(depth, held.shape[-1])
            start, size = (0 if v == 0 else run), (height if v == 1 else height + 1) * run
            q[pl.ds(0, size)] = jnp.dot(
                stacked[pl.ds(start, size)], kernel, preferred_element_type=jnp.float32
            )
        for r in range(height):
            here, after = pl.ds(r * run, run), pl.ds((r + 1) * run, run)
            middle = q1[here]
            rows[h, 0, pl.ds(pad + r * run, run)] = middle + q0[here] + q2[here]
            rows[h, 1, pl.ds(pad + r * run, run)] = middle + q0[after] + q2[after]

    column = lax.broadcasted_iota(jnp.int32, (width, 1), 0)
    for r in range(height):
        for s in range(2):
            for t in range(frames):
                at = pad + r * run + t * width
                left = jnp.where(column == 0, 0.0, rows[0, s, pl.ds(at - 1, width)])
                right = jnp.where(column == width - 1, 0.0, rows[2, s, pl.ds(at + 1, width)])
                base = rows[1, s, pl.ds(at, width)] + bias[...]
                even = base + left + rows[2, s, pl.ds(at, width)]
                odd = base + right + rows[0, s, pl.ds(at, width)]
                live = (t < count_here) & (r < length_here)
                slab = (2 * r + s) * frames + t
                even, odd = jnp.where(live, even, 0.0), jnp.where(live, odd, 0.0)
                for i in range(even.shape[-1] // LANES):
                    lanes = slice(i * LANES, (i + 1) * LANES)
                    woven[slab, i, pl.ds(0, width, 2)] = even[:, lanes]
                    woven[slab, i, pl.ds(1, width, 2)] = odd[:, lanes]
                    out[t, 2 * r + s, :, lanes] = woven[slab, i].astype(jnp.bfloat16)


def body(dims, features, frame_counts, row_lengths, norm_gain, norm_shift, conv_weight, conv_bias):
    frames, height, width, channels = features.shape
    made = conv_weight.shape[-1]
    size_x, size_y, size_z, n_tm, n_tile = dims
    anywhere = pl.BlockSpec(memory_space=pl.ANY)
    in_vmem = pl.BlockSpec(memory_space=pltpu.VMEM)
    in_smem = pl.BlockSpec(memory_space=pltpu.SMEM)
    bf16, f32 = jnp.bfloat16, jnp.float32
    halo = (frames + 2, width, channels)
    stats, prior, upper, lower = pl.pallas_call(
        functools.partial(exchange_kernel, dims),
        out_shape=(
            jax.ShapeDtypeStruct((8, channels), f32),
            jax.ShapeDtypeStruct((2, height, width, channels), bf16),
            jax.ShapeDtypeStruct(halo, bf16),
            jax.ShapeDtypeStruct(halo, bf16),
        ),
        in_specs=[anywhere] * 3,
        out_specs=(in_vmem, anywhere, anywhere, anywhere),
        scratch_shapes=[
            pltpu.VMEM(features.shape, bf16),
            pltpu.VMEM((2, height, width, channels), bf16),
            pltpu.VMEM(halo, bf16),
            pltpu.VMEM(halo, bf16),
            pltpu.VMEM((size_z * 2, 1, LANES), f32),
            pltpu.VMEM((size_x * size_y, 1, LANES), f32),
            pltpu.SMEM((1,), jnp.int32),
            pltpu.SMEM((1,), jnp.int32),
            pltpu.SemaphoreType.DMA((3,)),
            pltpu.SemaphoreType.DMA,
            pltpu.SemaphoreType.DMA,
            pltpu.SemaphoreType.DMA,
            pltpu.SemaphoreType.DMA((5,)),
        ],
        compiler_params=pltpu.CompilerParams(
            collective_id=0, has_side_effects=True, vmem_limit_bytes=16 * 1024 * 1024
        ),
        name="exchange",
    )(features, frame_counts, row_lengths)

    run = frames * width
    slots = height + 2
    return pl.pallas_call(
        functools.partial(convolve_kernel, n_tile),
        out_shape=jax.ShapeDtypeStruct((frames, 2 * height, 2 * width, made), bf16),
        in_specs=[anywhere] * 5 + [in_vmem] * 4 + [in_smem] * 2,
        out_specs=in_vmem,
        scratch_shapes=[
            pltpu.VMEM((slots, frames + 2, width, channels), bf16),
            pltpu.VMEM(((frames + 2) * width, channels), f32),
            pltpu.VMEM((slots * run, 3 * channels), bf16),
            pltpu.VMEM((9, 3, channels, made), bf16),
            pltpu.VMEM(((height + 1) * run, made), f32),
            pltpu.VMEM((height * run, made), f32),
            pltpu.VMEM(((height + 1) * run, made), f32),
            pltpu.VMEM((3, 2, height * run + 16, made), f32),
            pltpu.VMEM((2 * height * frames, made // LANES, 2 * width, LANES), f32),
            pltpu.SemaphoreType.DMA((2 * height + 2,)),
            pltpu.SemaphoreType.DMA((9,)),
        ],
        compiler_params=pltpu.CompilerParams(vmem_limit_bytes=VMEM_LIMIT),
        name="convolve",
    )(
        features, prior, upper, lower, conv_weight, stats,
        norm_gain.reshape(1, channels), norm_shift.reshape(1, channels),
        conv_bias.reshape(1, made), frame_counts, row_lengths,
    )


def factors(mesh):
    n_tm, n_tile = mesh.shape["tm"], mesh.shape["tile"]
    size_y = 1
    while size_y * size_y * 2 < n_tile:
        size_y *= 2
    return n_tm // 2, size_y, n_tile // size_y, n_tm, n_tile


def solution(mesh):
    in_specs = (P("tm", "tile", None, None), P("tm"), P("tile"), P(), P(), P(), P())
    out_specs = P("tm", "tile", None, None)
    return jax.shard_map(
        functools.partial(body, factors(mesh)),
        mesh=mesh, in_specs=in_specs, out_specs=out_specs, check_vma=False,
    )
```

time: 243 us -> 38.9 us (0.16)
  the two profiles are of different devices: /device:TPU:12 before, /device:TPU:1 now
where the time goes in v1:
time: 38.9 us; the launch traced here: 38.7 us
  Pallas kernels  33.8 us (87%)
  local copies, waits for them, and re-layouts  3.6 us (9%)
  between operations  1.33 us (3%)
    pallas_call x1, Pallas kernels, body(): pl.pallas_call(functools.partial(exchange_kernel, dims), out_shape=(jax.S...  19.3 us
    pallas_call x1, Pallas kernels, body(): pl.pallas_call(functools.partial(convolve_kernel, n_tile), out_shape=jax....  14.4 us
    unnamed x10, local copies, waits for them, and re-layouts  3.6 us

profile of v1, /device:TPU:1, one launch (start us, length us, event | category | flops | bytes accessed | tf_op | source)
XLA Modules:
  0.0 38.7 jit_solution(14218532383605405073)
XLA Ops:
  1.3 0.0 copy-start
  1.3 1.0 %copy-done = bf16[6,3,24,512]{3,2,1,0:T(8,128)(2,1)S(1)} copy-done((bf16[6,3,24,512]{3,2,1,0:T(8,128)(2,1)S(1)}, bf16[6,3,24,512]{3,2,1,0:T(8,128)(2,1)}, u32[]{:S(2)}) %copy-start) | copy-done | bytes 442392
  2.3 19.3 %exchange.1 = (f32[8,512]{1,0:T(8,128)S(1)}, bf16[2,3,24,512]{3,2,1,0:T(8,128)(2,1)S(1)}, bf16[8,24,512]{2,1,0:T(8,128)(2,1)S(1)}, bf16[8,24,512]{2,1,0:T(8,128)(2,1)S(1)}) custom-call(bf16[6,3,24,512]{3,2,1,0:T(8,128)(2,1)S(1)} %copy-done, s32[1]{0:T(128)S(6)} %copy.8.counts_in.counts, s32[1]{0:T(128)S(6)} %copy.9.lengths_in.lengths), custom_call_target="tpu_custom_call" | custom-call | tf_op jit(solution)/shard_map/exchange/pallas_call | solution.py:265
  21.6 0.0 copy-start.1
  21.6 0.7 %copy-done.1 = bf16[8,24,512]{2,1,0:T(8,128)(2,1)} copy-done((bf16[8,24,512]{2,1,0:T(8,128)(2,1)}, bf16[8,24,512]{2,1,0:T(8,128)(2,1)S(1)}, u32[]{:S(2)}) %copy-start.1) | copy-done | bytes 196632
  22.3 0.0 copy-start.2
  22.3 0.7 %copy-done.2 = bf16[8,24,512]{2,1,0:T(8,128)(2,1)} copy-done((bf16[8,24,512]{2,1,0:T(8,128)(2,1)}, bf16[8,24,512]{2,1,0:T(8,128)(2,1)S(1)}, u32[]{:S(2)}) %copy-start.2) | copy-done | bytes 196632
  23.0 0.0 copy-start.3
  23.0 0.7 %copy-done.3 = bf16[2,3,24,512]{3,2,1,0:T(8,128)(2,1)} copy-done((bf16[2,3,24,512]{3,2,1,0:T(8,128)(2,1)}, bf16[2,3,24,512]{3,2,1,0:T(8,128)(2,1)S(1)}, u32[]{:S(2)}) %copy-start.3) | copy-done | bytes 147480
  23.6 0.0 copy-start.4
  23.6 0.6 %copy-done.4 = f32[8,512]{1,0:T(8,128)} copy-done((f32[8,512]{1,0:T(8,128)}, f32[8,512]{1,0:T(8,128)S(1)}, u32[]{:S(2)}) %copy-start.4) | copy-done | bytes 16408
  24.2 14.4 %convolve.1 = bf16[6,6,48,256]{3,2,1,0:T(8,128)(2,1)} custom-call(bf16[6,3,24,512]{3,2,1,0:T(8,128)(2,1)} %features.3, bf16[2,3,24,512]{3,2,1,0:T(8,128)(2,1)} %copy-done.3, bf16[8,24,512]{2,1,0:T(8,128)(2,1)} %copy-done.1, bf16[8,24,512]{2,1,0:T(8,128)(2,1)} %copy-done.2, bf16[3,3,3,512,256]{4,3,2,1,0:T(8,128)(2,1)} %weights.1, f32[8,512]{1,0:T(8,128)} %copy-done.4, ...), custom_call_target="tpu_custom_call" | custom-call | tf_op jit(solution)/shard_map/convolve/pallas_call | solution.py:298
Async XLA Ops:
  1.3 1.0 %copy-start = (bf16[6,3,24,512]{3,2,1,0:T(8,128)(2,1)S(1)}, bf16[6,3,24,512]{3,2,1,0:T(8,128)(2,1)}, u32[]{:S(2)}) copy-start(bf16[6,3,24,512]{3,2,1,0:T(8,128)(2,1)} %features.3) | copy-start | bytes 1327108
  21.6 0.7 %copy-start.1 = (bf16[8,24,512]{2,1,0:T(8,128)(2,1)}, bf16[8,24,512]{2,1,0:T(8,128)(2,1)S(1)}, u32[]{:S(2)}) copy-start(bf16[8,24,512]{2,1,0:T(8,128)(2,1)S(1)} %get-tuple-element.10.upper) | copy-start | bytes 589828
  22.3 0.7 %copy-start.2 = (bf16[8,24,512]{2,1,0:T(8,128)(2,1)}, bf16[8,24,512]{2,1,0:T(8,128)(2,1)S(1)}, u32[]{:S(2)}) copy-start(bf16[8,24,512]{2,1,0:T(8,128)(2,1)S(1)} %get-tuple-element.11.lower) | copy-start | bytes 589828
  23.0 0.7 %copy-start.3 = (bf16[2,3,24,512]{3,2,1,0:T(8,128)(2,1)}, bf16[2,3,24,512]{3,2,1,0:T(8,128)(2,1)S(1)}, u32[]{:S(2)}) copy-start(bf16[2,3,24,512]{3,2,1,0:T(8,128)(2,1)S(1)} %get-tuple-element.9.prior) | copy-start | bytes 442372
  23.6 0.6 %copy-start.4 = (f32[8,512]{1,0:T(8,128)}, f32[8,512]{1,0:T(8,128)S(1)}, u32[]{:S(2)}) copy-start(f32[8,512]{1,0:T(8,128)S(1)} %get-tuple-element.12.stats) | copy-start | bytes 49156

commit v2 on v1

--- a/solution.py
+++ b/solution.py
@@ -11,7 +11,8 @@
 EPSILON = 1e-06
 MESH = pl.DeviceIdType.MESH
 LANES = 128
-VMEM_LIMIT = 56 * 1024 * 1024
+EXCHANGE_VMEM = 48 * 1024 * 1024
+CONVOLVE_VMEM = 40 * 1024 * 1024
 
 
 def group_matrix(channels, offset, transposed):
@@ -49,9 +50,9 @@
 
 
 def exchange_kernel(
-    dims, features, counts_in, lengths_in,
-    stats, prior, upper, lower,
-    block, tail, rising, sinking, first, second, counts, lengths,
+    dims, features, weights_in, gain_in, shift_in, bias_in, counts, lengths,
+    block, prior, upper, lower, stats, weights, gain, shift, bias,
+    tail, rising, sinking, first, second,
     local_sems, send_sem, first_sem, second_sem, halo_sems,
 ):
     size_x, size_y, size_z, n_tm, n_tile = dims
@@ -75,10 +76,6 @@
 
     load = pltpu.make_async_copy(features, block, local_sems.at[0])
     load.start()
-    load_counts = pltpu.make_async_copy(counts_in, counts, local_sems.at[1])
-    load_counts.start()
-    load_lengths = pltpu.make_async_copy(lengths_in, lengths, local_sems.at[2])
-    load_lengths.start()
 
     barrier = pltpu.get_barrier_semaphore()
     partners = [near(*s) for s in near_steps] + [far(*s) for s in far_steps]
@@ -86,8 +83,11 @@
     for partner in partners:
         pl.semaphore_signal(barrier, inc=1, device_id=partner, device_id_type=MESH)
 
-    load_counts.wait()
-    load_lengths.wait()
+    ahead = [(weights_in, weights), (gain_in, gain), (shift_in, shift), (bias_in, bias)]
+    ahead = [pltpu.make_async_copy(a, b, local_sems.at[1 + i]) for i, (a, b) in enumerate(ahead)]
+    for copy in ahead:
+        copy.start()
+
     load.wait()
     count_here = counts[0]
     length_here = lengths[0]
@@ -123,8 +123,6 @@
     first[0] = as_row(sums, spread, entries)
 
     pl.semaphore_wait(barrier, len(partners))
-
-    copies = []
 
     def send(source, target, sem, device):
         copy = pltpu.make_async_remote_copy(
@@ -158,6 +156,8 @@
     lane = lax.broadcasted_iota(jnp.int32, both.shape, 1)
     stats[...] = exact_dot(jnp.where(lane < GROUPS, both, 0.0), spread_out)
 
+    for copy in ahead:
+        copy.wait()
     for halo in halos:
         halo.wait_recv()
     sent = first.at[pl.ds(1, len(near_steps))]
@@ -169,10 +169,9 @@
 
 
 def convolve_kernel(
-    n_tile, features, prior, upper, lower, weights, stats, gain, shift, bias, counts, lengths,
+    n_tile, features, prior, upper, lower, stats, weights, gain, shift, bias, counts, lengths,
     out,
-    raw, hidden, stacked, held, q0, q1, q2, rows, woven,
-    raw_sem, weight_sems,
+    hidden, stacked, q0, q1, q2, rows, woven,
 ):
     frames, height, width, channels = features.shape
     slots = height + 2
@@ -180,35 +179,23 @@
     tm, tile = lax.axis_index("tm"), lax.axis_index("tile")
     count_here = counts[0]
     length_here = lengths[0]
-
-    loads = []
-    for r in range(height):
-        loads.append((features.at[:, r], raw.at[1 + r, pl.ds(2, frames)]))
-        loads.append((prior.at[:, r], raw.at[1 + r, pl.ds(0, 2)]))
-    loads.append((upper, raw.at[0]))
-    loads.append((lower, raw.at[slots - 1]))
-    loads = [pltpu.make_async_copy(a, b, raw_sem.at[i]) for i, (a, b) in enumerate(loads)]
-    for load in loads:
-        load.start()
-    order = [(v, h) for h in range(3) for v in range(3)]
-    fetches = {}
-    for v, h in order:
-        i = v * 3 + h
-        fetches[v, h] = pltpu.make_async_copy(weights.at[:, v, h], held.at[i], weight_sems.at[i])
-        fetches[v, h].start()
-    for load in loads:
-        load.wait()
-
     mean = stats[0:1]
     scale = stats[1:2] * gain[...]
     offset = shift[...]
     for slot in range(slots):
         is_lower = slot == length_here + 1
-        source = jnp.where(is_lower, slots - 1, slot)
         blank = (slot == 0) & (tile == 0) | is_lower & (tile == n_tile - 1)
         for k in range(frames + 2):
             frame = jnp.where(tm == 0, 2, k) if k < 2 else k
-            v = raw[source, frame].astype(jnp.float32)
+            if slot == 0: v = upper[frame]
+            elif slot == slots - 1: v = lower[frame]
+            else:
+                v = prior[k, slot - 1] if k < 2 else features[k - 2, slot - 1]
+                if k < 2:
+                    v = jnp.where(tm == 0, features[0, slot - 1], v)
+                if slot > 1:
+                    v = jnp.where(is_lower, lower[frame], v)
+            v = v.astype(jnp.float32)
             v = (v - mean) * scale + offset
             v = v / (1.0 + jnp.exp(-v))
             hidden[pl.ds(k * width, width)] = jnp.where(blank, 0.0, v)
@@ -220,9 +207,8 @@
     pad = 8
     for h in range(3):
         for v, q in enumerate((q0, q1, q2)):
-            fetches[v, h].wait()
             depth = 3 * channels
-            kernel = held[v * 3 + h].reshape(depth, held.shape[-1])
+            kernel = weights[:, v, h].reshape(depth, weights.shape[-1])
             start, size = (0 if v == 0 else run), (height if v == 1 else height + 1) * run
             q[pl.ds(0, size)] = jnp.dot(
                 stacked[pl.ds(start, size)], kernel, preferred_element_type=jnp.float32
@@ -257,69 +243,64 @@
     frames, height, width, channels = features.shape
     made = conv_weight.shape[-1]
     size_x, size_y, size_z, n_tm, n_tile = dims
+    run = frames * width
     anywhere = pl.BlockSpec(memory_space=pl.ANY)
     in_vmem = pl.BlockSpec(memory_space=pltpu.VMEM)
     in_smem = pl.BlockSpec(memory_space=pltpu.SMEM)
     bf16, f32 = jnp.bfloat16, jnp.float32
     halo = (frames + 2, width, channels)
-    stats, prior, upper, lower = pl.pallas_call(
+    ready = pl.pallas_call(
         functools.partial(exchange_kernel, dims),
         out_shape=(
-            jax.ShapeDtypeStruct((8, channels), f32),
-            jax.ShapeDtypeStruct((2, height, width, channels), bf16),
-            jax.ShapeDtypeStruct(halo, bf16),
-            jax.ShapeDtypeStruct(halo, bf16),
+            pltpu.VMEM(features.shape, bf16),
+            pltpu.VMEM((2, height, width, channels), bf16),
+            pltpu.VMEM(halo, bf16),
+            pltpu.VMEM(halo, bf16),
+            pltpu.VMEM((8, channels), f32),
+            pltpu.VMEM(conv_weight.shape, bf16),
+            pltpu.VMEM((1, channels), f32),
+            pltpu.VMEM((1, channels), f32),
+            pltpu.VMEM((1, made), f32),
         ),
-        in_specs=[anywhere] * 3,
-        out_specs=(in_vmem, anywhere, anywhere, anywhere),
+        in_specs=[anywhere] * 5 + [in_smem] * 2,
+        out_specs=(in_vmem,) * 9,
         scratch_shapes=[
-            pltpu.VMEM(features.shape, bf16),
             pltpu.VMEM((2, height, width, channels), bf16),
             pltpu.VMEM(halo, bf16),
             pltpu.VMEM(halo, bf16),
             pltpu.VMEM((size_z * 2, 1, LANES), f32),
             pltpu.VMEM((size_x * size_y, 1, LANES), f32),
-            pltpu.SMEM((1,), jnp.int32),
-            pltpu.SMEM((1,), jnp.int32),
-            pltpu.SemaphoreType.DMA((3,)),
+            pltpu.SemaphoreType.DMA((5,)),
             pltpu.SemaphoreType.DMA,
             pltpu.SemaphoreType.DMA,
             pltpu.SemaphoreType.DMA,
             pltpu.SemaphoreType.DMA((5,)),
         ],
         compiler_params=pltpu.CompilerParams(
-            collective_id=0, has_side_effects=True, vmem_limit_bytes=16 * 1024 * 1024
+            collective_id=0, has_side_effects=True, vmem_limit_bytes=EXCHANGE_VMEM
         ),
         name="exchange",
-    )(features, frame_counts, row_lengths)
-
-    run = frames * width
-    slots = height + 2
+    )(
+        features, conv_weight, norm_gain.reshape(1, channels), norm_shift.reshape(1, channels),
+        conv_bias.reshape(1, made), frame_counts, row_lengths,
+    )
     return pl.pallas_call(
         functools.partial(convolve_kernel, n_tile),
         out_shape=jax.ShapeDtypeStruct((frames, 2 * height, 2 * width, made), bf16),
-        in_specs=[anywhere] * 5 + [in_vmem] * 4 + [in_smem] * 2,
+        in_specs=[in_vmem] * 9 + [in_smem] * 2,
         out_specs=in_vmem,
         scratch_shapes=[
-            pltpu.VMEM((slots, frames + 2, width, channels), bf16),
             pltpu.VMEM(((frames + 2) * width, channels), f32),
-            pltpu.VMEM((slots * run, 3 * channels), bf16),
-            pltpu.VMEM((9, 3, channels, made), bf16),
+            pltpu.VMEM(((height + 2) * run, 3 * channels), bf16),
             pltpu.VMEM(((height + 1) * run, made), f32),
             pltpu.VMEM((height * run, made), f32),
             pltpu.VMEM(((height + 1) * run, made), f32),
             pltpu.VMEM((3, 2, height * run + 16, made), f32),
             pltpu.VMEM((2 * height * frames, made // LANES, 2 * width, LANES), f32),
-            pltpu.SemaphoreType.DMA((2 * height + 2,)),
-            pltpu.SemaphoreType.DMA((9,)),
         ],
-        compiler_params=pltpu.CompilerParams(vmem_limit_bytes=VMEM_LIMIT),
+        compiler_params=pltpu.CompilerParams(vmem_limit_bytes=CONVOLVE_VMEM),
         name="convolve",
-    )(
-        features, prior, upper, lower, conv_weight, stats,
-        norm_gain.reshape(1, channels), norm_shift.reshape(1, channels),
-        conv_bias.reshape(1, made), frame_counts, row_lengths,
-    )
+    )(*ready, frame_counts, row_lengths)
 
 
 def factors(mesh):

time: 38.9 us -> 26.3 us (0.68)
  Pallas kernels: 33.8 us -> 24.8 us
  local copies, waits for them, and re-layouts: 3.6 us -> 0 us
    pallas_call x1, Pallas kernels: 14.4 us -> 5.6 us  [body(): pl.pallas_call(functools.partial(convolve_kernel, n_tile), out_shape=jax....]
    unnamed x10 -> x0, local copies, waits for them, and re-layouts: 3.6 us -> none
where the time goes in v2:
time: 26.3 us; the launch traced here: 26.2 us
  Pallas kernels  24.8 us (94%)
  between operations  1.31 us (5%)
    pallas_call x1, Pallas kernels, body(): pl.pallas_call(functools.partial(exchange_kernel, dims), out_shape=(pltpu...  19.3 us
    pallas_call x1, Pallas kernels, body(): pl.pallas_call(functools.partial(convolve_kernel, n_tile), out_shape=jax....  5.6 us

profile of v2, /device:TPU:1, one launch (start us, length us, event | category | flops | bytes accessed | tf_op | source)
XLA Modules:
  0.0 26.2 jit_solution(15087603224880313571)
XLA Ops:
  1.3 19.3 %exchange.1 = (bf16[6,3,24,512]{3,2,1,0:T(8,128)(2,1)S(1)}, bf16[2,3,24,512]{3,2,1,0:T(8,128)(2,1)S(1)}, bf16[8,24,512]{2,1,0:T(8,128)(2,1)S(1)}, bf16[8,24,512]...) custom-call(bf16[6,3,24,512]{3,2,1,0:T(8,128)(2,1)} %features.1, ...), custom_call_target="tpu_custom_call" | custom-call | tf_op jit(solution)/shard_map/exchange/pallas_call | solution.py:252
  20.6 5.6 %convolve.1 = bf16[6,6,48,256]{3,2,1,0:T(8,128)(2,1)} custom-call(bf16[6,3,24,512]{3,2,1,0:T(8,128)(2,1)S(1)} %get-tuple-element.14.features, bf16[2,3,24,512]{3,2,1,0:T(8,128)(2,1)S(1)} %get-tuple-element.15.prior, bf16[8,24,512]{2,1,0:T(8,128)(2,1)S(1)} %get-tuple-element.16.upper, bf16[8,24,512]{2,1,0:T(8,128)(2,1)S(1)} %get-tuple-element.17.lower, ...), custom_call_target="tpu_custom_call" | custom-call | tf_op jit(solution)/shard_map/convolve/pallas_call | solution.py:287

commit v3 on v2

v3 whole, which is shorter than its diff:
```python
import functools

import jax
import jax.numpy as jnp
from jax import lax
from jax.experimental import pallas as pl
from jax.experimental.pallas import tpu as pltpu
from jax.sharding import PartitionSpec as P

GROUPS = 32
EPSILON = 1e-06
MESH = pl.DeviceIdType.MESH
LANES = 128
EXCHANGE_VMEM = 48 * 1024 * 1024
CONVOLVE_VMEM = 40 * 1024 * 1024


def group_matrix(channels, offset, transposed):
    span = channels // GROUPS
    shape = (LANES, channels) if transposed else (channels, LANES)
    channel = lax.broadcasted_iota(jnp.int32, shape, 1 if transposed else 0)
    lane = lax.broadcasted_iota(jnp.int32, shape, 0 if transposed else 1)
    low = (lane - offset) * span
    return ((channel >= low) & (channel < low + span)).astype(jnp.float32)


def exact_dot(a, one_hot):
    high = a.astype(jnp.bfloat16).astype(jnp.float32)
    rest = a - high
    middle = rest.astype(jnp.bfloat16).astype(jnp.float32)
    terms = jnp.concatenate([high, middle, rest - middle, jnp.zeros_like(a)], 0).astype(jnp.bfloat16)
    out = jnp.dot(terms, one_hot.astype(jnp.bfloat16), preferred_element_type=jnp.float32)
    return out[:8] + out[8:16] + out[16:24]


def merge(rows):
    totals = functools.reduce(lambda a, b: a + b, rows)
    counts = [pltpu.roll(row, LANES - 2 * GROUPS, 1) for row in rows]
    entries = pltpu.roll(totals, LANES - 2 * GROUPS, 1)
    mean = totals / entries
    between = jnp.zeros_like(totals)
    for row, count in zip(rows, counts):
        off = row / count - mean
        between = between + count * (off * off)
    spread = pltpu.roll(totals, LANES - GROUPS, 1) + between
    return totals, spread, entries


def as_row(totals, spread, entries):
    lane = lax.broadcasted_iota(jnp.int32, totals.shape, 1)
    spread = pltpu.roll(spread, GROUPS, 1)
    entries = pltpu.roll(entries, 2 * GROUPS, 1)
    row = jnp.where(lane < GROUPS, totals, jnp.where(lane < 2 * GROUPS, spread, entries))
    return jnp.where(lane < 3 * GROUPS, row, 1.0)


def exchange_kernel(
    dims, features, weights_in, gain_in, shift_in, bias_in, counts, lengths,
    block, prior, upper, lower, stats, weights, gain, shift, bias,
    tail, rising, sinking, row, first, second, result,
    local_sems, row_send, first_sem, second_send, second_sem, result_send, result_sem,
    halo_send, halo_sems,
):
    size_x, size_y, size_z, n_tm, n_tile = dims
    frames, height, width, channels = block.shape
    tm, tile = lax.axis_index("tm"), lax.axis_index("tile")
    x, core = tm // 2, tm % 2
    y, z = tile // size_z, tile % size_z
    planes, half = size_z // 2, size_z // 4
    gathers = z < planes
    serves = ((z == 1) | (z == planes - 1)) & (core == 1)
    server = jnp.where(z < planes + half, planes - 1, 1)

    def column(other_z, other_core):
        return x * 2 + other_core, y * size_z + other_z

    def far(dx, dy):
        return ((x + dx) % size_x) * 2 + core, ((y + dy) % size_y) * size_z + z

    def beside(dt, dr):
        return (tm + dt + n_tm) % n_tm, (tile + dr + n_tile) % n_tile

    far_steps = [(dx, dy) for dx in range(size_x) for dy in range(size_y)][1:]
    halo_steps = [(a, b) for a in (-1, 0, 1) for b in (-1, 0, 1) if (a, b) != (0, 0)]
    n_column, n_gather = 2 * size_z, 2 * planes

    load = pltpu.make_async_copy(features, block, local_sems.at[0])
    load.start()

    barrier = pltpu.get_barrier_semaphore()

    def greet(device):
        pl.semaphore_signal(barrier, inc=1, device_id=device, device_id_type=MESH)

    for step in halo_steps:
        greet(beside(*step))

    @pl.when(gathers)
    def _():
        for dz in range(size_z):
            for dc in range(2):
                if dz + dc:
                    greet(column((z + dz) % size_z, (core + dc) % 2))
        for step in far_steps:
            greet(far(*step))

    @pl.when(jnp.logical_not(gathers))
    def _():
        greet(column(server, 1))

    ahead = [(weights_in, weights), (gain_in, gain), (shift_in, shift), (bias_in, bias)]
    ahead = [pltpu.make_async_copy(a, b, local_sems.at[1 + i]) for i, (a, b) in enumerate(ahead)]
    for copy in ahead:
        copy.start()

    load.wait()
    count_here = counts[0]
    length_here = lengths[0]

    cells = (count_here * length_here * (width * (channels // GROUPS))).astype(jnp.float32)
    spread_out = group_matrix(channels, 0, True)
    gather = group_matrix(channels, 0, False)

    def over_live(term):
        total = jnp.zeros((8, channels), jnp.float32)
        for f in range(frames):
            for r in range(height):
                live = (f < count_here) & (r < length_here)
                part = term(block[f, r].astype(jnp.float32))
                part = jnp.where(live, part, 0.0)
                total = total + sum(part[8 * i : 8 * i + 8] for i in range(width // 8))
        return jnp.sum(exact_dot(total, gather), axis=0, keepdims=True)

    sums = over_live(lambda v: v)
    centre = exact_dot(jnp.broadcast_to(sums / cells, (8, LANES)), spread_out)[:1]
    spread = over_live(lambda v: (v - centre) * (v - centre))
    entries = jnp.zeros_like(sums) + cells
    row[0] = as_row(sums, spread, entries)
    own = z * 2 + core

    def send_row(device):
        pltpu.make_async_remote_copy(
            src_ref=row.at[0], dst_ref=first.at[own], send_sem=row_send, recv_sem=first_sem,
            device_id=device, device_id_type=MESH,
        ).start()

    @pl.when(gathers)
    def _():
        known = n_gather - 1 + len(far_steps) + len(halo_steps)
        pl.semaphore_wait(barrier, known + jnp.where(serves, 4, 0))
        first[own] = row[0]
        for dz in range(planes):
            for dc in range(2):
                if dz + dc:
                    send_row(column((z + dz) % planes, (core + dc) % 2))

    @pl.when(jnp.logical_not(gathers))
    def _():
        pl.semaphore_wait(barrier, n_gather + len(halo_steps))
        for to_z in range(planes):
            for to_core in range(2):
                send_row(column(to_z, to_core))

    recent = jnp.maximum(count_here - 2, 0)
    last_row = jnp.maximum(length_here - 1, 0)
    for k in range(2):
        tail[k] = block[recent + k]
        rising[k] = tail[k, last_row]
        sinking[k] = tail[k, 0]
    for k in range(frames):
        rising[2 + k] = block[k, last_row]
        sinking[2 + k] = block[k, 0]
    here, before = pl.ds(2, frames), pl.ds(0, 2)
    halos = [
        (rising.at[here], upper.at[here], (0, 1)),
        (sinking.at[here], lower.at[here], (0, -1)),
        (rising.at[before], upper.at[before], (1, 1)),
        (sinking.at[before], lower.at[before], (1, -1)),
        (tail, prior, (1, 0)),
    ]
    halos = [
        pltpu.make_async_remote_copy(
            src_ref=source, dst_ref=target, send_sem=halo_send.at[i], recv_sem=halo_sems.at[i],
            device_id=beside(*step), device_id_type=MESH,
        )
        for i, (source, target, step) in enumerate(halos)
    ]
    for halo in halos:
        halo.start()
    widen = group_matrix(channels, 0, True) + group_matrix(channels, GROUPS, True)

    def answers():
        base = jnp.where(z == 1, planes + half, planes)
        return [
            pltpu.make_async_remote_copy(
                src_ref=result.at[0], dst_ref=result.at[0], send_sem=result_send.at[k],
                recv_sem=result_sem, device_id=column(base + k // 2, k % 2), device_id_type=MESH,
            )
            for k in range(4)
        ]

    @pl.when(gathers)
    def _():
        sent = first.at[pl.ds(0, n_gather - 1)]
        pltpu.make_async_copy(sent, sent, row_send).wait()
        arrived = first.at[pl.ds(0, n_column - 1)]
        pltpu.make_async_copy(arrived, arrived, first_sem).wait()
        second[0] = as_row(*merge([first[i] for i in range(n_column)]))
        copies = [
            pltpu.make_async_remote_copy(
                src_ref=second.at[0], dst_ref=second.at[1 + i], send_sem=second_send,
                recv_sem=second_sem, device_id=far(*step), device_id_type=MESH,
            )
            for i, step in enumerate(far_steps)
        ]
        for copy in copies:
            copy.start()
        for copy in ahead:
            copy.wait()
        for halo in halos:
            halo.wait()
        sent = second.at[pl.ds(1, len(far_steps))]
        pltpu.make_async_copy(sent, sent, second_send).wait()
        pltpu.make_async_copy(sent, sent, second_sem).wait()
        totals, spread, entries = merge([second[i] for i in range(1 + len(far_steps))])
        mean = totals / entries
        scale = lax.rsqrt(spread / entries + EPSILON)
        lane = lax.broadcasted_iota(jnp.int32, mean.shape, 1)
        result[0] = jnp.where(lane < GROUPS, mean, pltpu.roll(scale, GROUPS, 1))

        @pl.when(serves)
        def _():
            for answer in answers():
                answer.start()

    @pl.when(jnp.logical_not(gathers))
    def _():
        sent = first.at[pl.ds(0, n_gather)]
        pltpu.make_async_copy(sent, sent, row_send).wait()
        for copy in ahead:
            copy.wait()
        for halo in halos:
            halo.wait()
        pltpu.make_async_copy(result.at[0], result.at[0], result_sem).wait()

    both = jnp.broadcast_to(result[0], (8, LANES))
    lane = lax.broadcasted_iota(jnp.int32, both.shape, 1)
    sub = lax.broadcasted_iota(jnp.int32, both.shape, 0)
    stats[...] = exact_dot(jnp.where(lane // GROUPS == sub, both, 0.0), widen)

    @pl.when(serves)
    def _():
        for answer in answers():
            answer.wait_send()


def convolve_kernel(
    n_tile, features, prior, upper, lower, stats, weights, gain, shift, bias, counts, lengths,
    out_hbm,
    out, stacked, q0, q1, q2, woven, hidden, out_sems,
):
    frames, height, width, channels = features.shape
    slots, run, depth = height + 2, frames * width, 3 * channels
    products = (q0, q1, q2)
    tm, tile = lax.axis_index("tm"), lax.axis_index("tile")
    count_here = counts[0]
    length_here = lengths[0]
    mean = stats[0:1]
    scale = stats[1:2] * gain[...]
    offset = shift[...]
    column = lax.broadcasted_iota(jnp.int32, (width, 1), 0)

    def normalise(slot, k):
        is_lower = slot == length_here + 1
        blank = (slot == 0) & (tile == 0) | is_lower & (tile == n_tile - 1)
        frame = jnp.where(tm == 0, 2, k) if k < 2 else k
        if slot == 0:
            v = upper[frame]
        elif slot == slots - 1:
            v = lower[frame]
        else:
            v = prior[k, slot - 1] if k < 2 else features[k - 2, slot - 1]
            if k < 2:
                v = jnp.where(tm == 0, features[0, slot - 1], v)
            if slot > 1:
                v = jnp.where(is_lower, lower[frame], v)
        v = v.astype(jnp.float32)
        v = (v - mean) * scale + offset
        v = v / (1.0 + jnp.exp(-v))
        hidden[slot % 2, pl.ds(k * width, width)] = jnp.where(blank, 0.0, v)

    def stack(slot, a):
        stacked[pl.ds(slot * run, run), pl.ds(a * channels, channels)] = hidden[
            slot % 2, pl.ds(a * width, run)
        ].astype(jnp.bfloat16)

    def multiply(slot, h, v):
        kernel = weights[:, v, h].reshape(depth, weights.shape[-1])
        products[v][h, slot] = jnp.dot(
            stacked[pl.ds(slot * run, run)], kernel, preferred_element_type=jnp.float32
        )

    def finish(r, s, t):
        at = pl.ds(t * width, width)
        first, middle, last = [
            q0[h, r + s, at] + q1[h, r + 1, at] + q2[h, r + 1 + s, at] for h in range(3)
        ]
        middle = middle + bias[...]
        left = jnp.where(column == 0, 0.0, pltpu.roll(first, 1, 0))
        right = jnp.where(column == width - 1, 0.0, pltpu.roll(last, width - 1, 0))
        live = (t < count_here) & (r < length_here)
        even = jnp.where(live, middle + left + last, 0.0)
        odd = jnp.where(live, middle + right + first, 0.0)
        slab = (2 * r + s) * frames + t
        for i in range(even.shape[-1] // LANES):
            lanes = slice(i * LANES, (i + 1) * LANES)
            woven[slab, i, pl.ds(0, width, 2)] = even[:, lanes]
            woven[slab, i, pl.ds(1, width, 2)] = odd[:, lanes]
            out[t, 2 * r + s, :, lanes] = woven[slab, i].astype(jnp.bfloat16)

    def leave(row):
        return pltpu.make_async_copy(out.at[:, row], out_hbm.at[:, row], out_sems.at[row])

    def preparing(slot):
        work = [functools.partial(normalise, slot, k) for k in range(frames + 2)]
        return work + [functools.partial(stack, slot, a) for a in range(3)]

    def finishing(r, s):
        work = [functools.partial(finish, r, s, t) for t in range(frames)]
        return work + [lambda: leave(2 * r + s).start()]

    for piece in preparing(0):
        piece()
    for slot in range(slots):
        beside = preparing(slot + 1) if slot + 1 < slots else []
        if 2 <= slot:
            beside = beside + finishing(slot - 2, 0)
        if 3 <= slot:
            beside = finishing(slot - 3, 1) + beside
        taps = [
            (h, v) for h in range(3) for v in range(3)
            if not (slot == 0 and v > 0 or slot == slots - 1 and v < 2)
        ]
        done = 0
        for i, (h, v) in enumerate(taps):
            multiply(slot, h, v)
            upto = len(beside) * (i + 1) // len(taps)
            for piece in beside[done:upto]:
                piece()
            done = upto
    for piece in finishing(height - 1, 1):
        piece()
    for row in range(2 * height):
        leave(row).wait()


def body(dims, features, frame_counts, row_lengths, norm_gain, norm_shift, conv_weight, conv_bias):
    frames, height, width, channels = features.shape
    made = conv_weight.shape[-1]
    size_x, size_y, size_z, n_tm, n_tile = dims
    run = frames * width
    anywhere = pl.BlockSpec(memory_space=pl.ANY)
    in_vmem = pl.BlockSpec(memory_space=pltpu.VMEM)
    in_smem = pl.BlockSpec(memory_space=pltpu.SMEM)
    bf16, f32 = jnp.bfloat16, jnp.float32
    halo = (frames + 2, width, channels)
    ready = pl.pallas_call(
        functools.partial(exchange_kernel, dims),
        out_shape=(
            pltpu.VMEM(features.shape, bf16),
            pltpu.VMEM((2, height, width, channels), bf16),
            pltpu.VMEM(halo, bf16),
            pltpu.VMEM(halo, bf16),
            pltpu.VMEM((8, channels), f32),
            pltpu.VMEM(conv_weight.shape, bf16),
            pltpu.VMEM((1, channels), f32),
            pltpu.VMEM((1, channels), f32),
            pltpu.VMEM((1, made), f32),
        ),
        in_specs=[anywhere] * 5 + [in_smem] * 2,
        out_specs=(in_vmem,) * 9,
        scratch_shapes=[
            pltpu.VMEM((2, height, width, channels), bf16),
            pltpu.VMEM(halo, bf16),
            pltpu.VMEM(halo, bf16),
            pltpu.VMEM((1, 1, LANES), f32),
            pltpu.VMEM((size_z * 2, 1, LANES), f32),
            pltpu.VMEM((size_x * size_y, 1, LANES), f32),
            pltpu.VMEM((1, 1, LANES), f32),
            pltpu.SemaphoreType.DMA((5,)),
            pltpu.SemaphoreType.DMA,
            pltpu.SemaphoreType.DMA,
            pltpu.SemaphoreType.DMA,
            pltpu.SemaphoreType.DMA,
            pltpu.SemaphoreType.DMA((4,)),
            pltpu.SemaphoreType.DMA,
            pltpu.SemaphoreType.DMA((5,)),
            pltpu.SemaphoreType.DMA((5,)),
        ],
        compiler_params=pltpu.CompilerParams(
            collective_id=0, has_side_effects=True, vmem_limit_bytes=EXCHANGE_VMEM
        ),
        name="exchange",
    )(
        features, conv_weight, norm_gain.reshape(1, channels), norm_shift.reshape(1, channels),
        conv_bias.reshape(1, made), frame_counts, row_lengths,
    )
    return pl.pallas_call(
        functools.partial(convolve_kernel, n_tile),
        out_shape=jax.ShapeDtypeStruct((frames, 2 * height, 2 * width, made), bf16),
        in_specs=[in_vmem] * 9 + [in_smem] * 2,
        out_specs=anywhere,
        scratch_shapes=[
            pltpu.VMEM((frames, 2 * height, 2 * width, made), bf16),
            pltpu.VMEM(((height + 2) * run, 3 * channels), bf16),
            pltpu.VMEM((3, height + 2, run, made), f32),
            pltpu.VMEM((3, height + 2, run, made), f32),
            pltpu.VMEM((3, height + 2, run, made), f32),
            pltpu.VMEM((2 * height * frames, made // LANES, 2 * width, LANES), f32),
            pltpu.VMEM((2, (frames + 2) * width, channels), f32),
            pltpu.SemaphoreType.DMA((2 * height,)),
        ],
        compiler_params=pltpu.CompilerParams(vmem_limit_bytes=CONVOLVE_VMEM),
        name="convolve",
    )(*ready, frame_counts, row_lengths)


def factors(mesh):
    n_tm, n_tile = mesh.shape["tm"], mesh.shape["tile"]
    size_y = 1
    while size_y * size_y * 2 < n_tile:
        size_y *= 2
    return n_tm // 2, size_y, n_tile // size_y, n_tm, n_tile


def solution(mesh):
    in_specs = (P("tm", "tile", None, None), P("tm"), P("tile"), P(), P(), P(), P())
    out_specs = P("tm", "tile", None, None)
    return jax.shard_map(
        functools.partial(body, factors(mesh)),
        mesh=mesh, in_specs=in_specs, out_specs=out_specs, check_vma=False,
    )
```

time: 26.3 us -> 25.3 us (0.962)
  Pallas kernels: 24.8 us -> 23.9 us
    pallas_call x1, Pallas kernels: 19.3 us -> 18.7 us  [body(): pl.pallas_call(functools.partial(exchange_kernel, dims), out_shape=(pltpu...]
    pallas_call x1, Pallas kernels: 5.6 us -> 5.23 us  [body(): pl.pallas_call(functools.partial(convolve_kernel, n_tile), out_shape=jax....]
where the time goes in v3:
time: 25.3 us; the launch traced here: 25.2 us
  Pallas kernels  23.9 us (94%)
  between operations  1.31 us (5%)
    pallas_call x1, Pallas kernels, body(): pl.pallas_call(functools.partial(exchange_kernel, dims), out_shape=(pltpu...  18.7 us
    pallas_call x1, Pallas kernels, body(): pl.pallas_call(functools.partial(convolve_kernel, n_tile), out_shape=jax....  5.23 us

profile of v3, /device:TPU:1, one launch (start us, length us, event | category | flops | bytes accessed | tf_op | source)
XLA Modules:
  0.0 25.2 jit_solution(1755998084255103032)
XLA Ops:
  1.3 18.7 %exchange.1 = (bf16[6,3,24,512]{3,2,1,0:T(8,128)(2,1)S(1)}, bf16[2,3,24,512]{3,2,1,0:T(8,128)(2,1)S(1)}, bf16[8,24,512]{2,1,0:T(8,128)(2,1)S(1)}, bf16[8,24,512]...) custom-call(bf16[6,3,24,512]{3,2,1,0:T(8,128)(2,1)} %features.1, ...), custom_call_target="tpu_custom_call" | custom-call | tf_op jit(solution)/shard_map/exchange/pallas_call | solution.py:367
  20.0 5.2 %convolve.1 = bf16[6,6,48,256]{3,2,1,0:T(8,128)(2,1)} custom-call(bf16[6,3,24,512]{3,2,1,0:T(8,128)(2,1)S(1)} %get-tuple-element.14.features, bf16[2,3,24,512]{3,2,1,0:T(8,128)(2,1)S(1)} %get-tuple-element.15.prior, bf16[8,24,512]{2,1,0:T(8,128)(2,1)S(1)} %get-tuple-element.16.upper, bf16[8,24,512]{2,1,0:T(8,128)(2,1)S(1)} %get-tuple-element.17.lower, ...), custom_call_target="tpu_custom_call" | custom-call | tf_op jit(solution)/shard_map/convolve/pallas_call | solution.py:408

commit v4 on v3

--- a/solution.py
+++ b/solution.py
@@ -8,6 +8,7 @@
 from jax.sharding import PartitionSpec as P
 
 GROUPS = 32
+REACH = 1
 EPSILON = 1e-06
 MESH = pl.DeviceIdType.MESH
 LANES = 128
@@ -34,32 +35,32 @@
 
 
 def merge(rows):
-    totals = functools.reduce(lambda a, b: a + b, rows)
-    counts = [pltpu.roll(row, LANES - 2 * GROUPS, 1) for row in rows]
-    entries = pltpu.roll(totals, LANES - 2 * GROUPS, 1)
-    mean = totals / entries
-    between = jnp.zeros_like(totals)
-    for row, count in zip(rows, counts):
-        off = row / count - mean
-        between = between + count * (off * off)
-    spread = pltpu.roll(totals, LANES - GROUPS, 1) + between
-    return totals, spread, entries
-
-
-def as_row(totals, spread, entries):
+    totals = jnp.sum(rows, axis=0, keepdims=True)
+    entries = pltpu.roll(totals, 3 * GROUPS, 1)
+    mean = pltpu.roll(totals, 2 * GROUPS, 1) / entries
+    off = rows - mean
+    between = jnp.sum(pltpu.roll(rows, 3 * GROUPS, 1) * (off * off), axis=0, keepdims=True)
+    return totals, mean, pltpu.roll(totals, GROUPS, 1) + between, entries
+
+
+def as_row(totals, mean, spread):
     lane = lax.broadcasted_iota(jnp.int32, totals.shape, 1)
-    spread = pltpu.roll(spread, GROUPS, 1)
-    entries = pltpu.roll(entries, 2 * GROUPS, 1)
-    row = jnp.where(lane < GROUPS, totals, jnp.where(lane < 2 * GROUPS, spread, entries))
-    return jnp.where(lane < 3 * GROUPS, row, 1.0)
+    row = jnp.where(lane // GROUPS == 1, pltpu.roll(spread, 3 * GROUPS, 1), totals)
+    return jnp.where(lane // GROUPS == 2, mean, row)
+
+
+def as_result(totals, mean, spread, entries):
+    scale = lax.rsqrt(spread / entries + EPSILON)
+    lane = lax.broadcasted_iota(jnp.int32, totals.shape, 1)
+    return jnp.where(lane < 3 * GROUPS, mean, pltpu.roll(scale, GROUPS, 1))
 
 
 def exchange_kernel(
     dims, features, weights_in, gain_in, shift_in, bias_in, counts, lengths,
-    block, prior, upper, lower, stats, weights, gain, shift, bias,
-    tail, rising, sinking, row, first, second, result,
-    local_sems, row_send, first_sem, second_send, second_sem, result_send, result_sem,
-    halo_send, halo_sems,
+    block, halo, stats, weights, gain, shift, bias,
+    leaving, row, first, second, table, result,
+    load_sem, weight_sem, row_send, direct_send, direct_sem, first_sem, second_send, second_sem,
+    result_send, result_sem, halo_send, halo_sem,
 ):
     size_x, size_y, size_z, n_tm, n_tile = dims
     frames, height, width, channels = block.shape
@@ -80,11 +81,29 @@
     def beside(dt, dr):
         return (tm + dt + n_tm) % n_tm, (tile + dr + n_tile) % n_tile
 
+    def is_early(at_x, at_y, at_z):
+        off_x = jnp.where(at_x > size_x // 2, size_x - at_x, at_x)
+        off_y = jnp.where(at_y > size_y // 2, size_y - at_y, at_y)
+        return off_x + off_y + at_z <= REACH
+
+    early = is_early(x, y, z)
+    direct = []
+    for reach in range(REACH + 1):
+        for at_z in range(size_z):
+            for at_y in range(size_y):
+                for at_x in range(size_x):
+                    off = min(at_x, size_x - at_x) + min(at_y, size_y - at_y) + at_z
+                    if off == reach:
+                        place = at_y * size_z + at_z
+                        direct = direct + [(2 * at_x + 1, place), (2 * at_x, place)]
+    rank = tile * n_tm + tm
+    n_devices = n_tm * n_tile
+
     far_steps = [(dx, dy) for dx in range(size_x) for dy in range(size_y)][1:]
     halo_steps = [(a, b) for a in (-1, 0, 1) for b in (-1, 0, 1) if (a, b) != (0, 0)]
     n_column, n_gather = 2 * size_z, 2 * planes
 
-    load = pltpu.make_async_copy(features, block, local_sems.at[0])
+    load = pltpu.make_async_copy(features, block, load_sem)
     load.start()
 
     barrier = pltpu.get_barrier_semaphore()
@@ -108,10 +127,20 @@
     def _():
         greet(column(server, 1))
 
-    ahead = [(weights_in, weights), (gain_in, gain), (shift_in, shift), (bias_in, bias)]
-    ahead = [pltpu.make_async_copy(a, b, local_sems.at[1 + i]) for i, (a, b) in enumerate(ahead)]
-    for copy in ahead:
-        copy.start()
+    @pl.when(early)
+    def _():
+        by_tm = [(tm + i) % n_tm for i in range(n_tm)]
+        by_y = [(y + i) % size_y * size_z for i in range(size_y)]
+        by_z = [(z + i) % size_z for i in range(size_z)]
+        for dz in sorted(range(size_z), key=lambda i: abs(2 * i - size_z)):
+            for dy in sorted(range(size_y), key=lambda i: abs(2 * i - size_y)):
+                place = by_y[dy] + by_z[dz]
+                for dt in sorted(range(n_tm), key=lambda i: abs(2 * i - n_tm)):
+                    if dz + dy + dt:
+                        greet((by_tm[dt], place))
+
+    fetch = pltpu.make_async_copy(weights_in, weights, weight_sem)
+    fetch.start()
 
     load.wait()
     count_here = counts[0]
@@ -134,8 +163,10 @@
     sums = over_live(lambda v: v)
     centre = exact_dot(jnp.broadcast_to(sums / cells, (8, LANES)), spread_out)[:1]
     spread = over_live(lambda v: (v - centre) * (v - centre))
-    entries = jnp.zeros_like(sums) + cells
-    row[0] = as_row(sums, spread, entries)
+    lane = lax.broadcasted_iota(jnp.int32, sums.shape, 1)
+    packed = jnp.where(lane < GROUPS, sums, pltpu.roll(spread, GROUPS, 1))
+    means = pltpu.roll(sums / cells, 2 * GROUPS, 1)
+    row[0] = jnp.where(lane < 2 * GROUPS, packed, jnp.where(lane < 3 * GROUPS, means, cells))
     own = z * 2 + core
 
     def send_row(device):
@@ -144,10 +175,29 @@
             device_id=device, device_id_type=MESH,
         ).start()
 
+    def to_early(device):
+        return pltpu.make_async_remote_copy(
+            src_ref=row.at[0], dst_ref=table.at[rank], send_sem=direct_send,
+            recv_sem=direct_sem, device_id=device, device_id_type=MESH,
+        )
+
+    def send_early():
+        for device in direct:
+            @pl.when(jnp.logical_not((tm == device[0]) & (tile == device[1])))
+            def _():
+                to_early(device).start()
+
+    def sent_early(count):
+        sent = table.at[pl.ds(0, count)]
+        pltpu.make_async_copy(sent, sent, direct_send).wait()
+
+    others = len(direct) - jnp.where(early, 1, 0)
+
     @pl.when(gathers)
     def _():
         known = n_gather - 1 + len(far_steps) + len(halo_steps)
-        pl.semaphore_wait(barrier, known + jnp.where(serves, 4, 0))
+        pl.semaphore_wait(barrier, known + others + jnp.where(serves, 4, 0))
+        send_early()
         first[own] = row[0]
         for dz in range(planes):
             for dc in range(2):
@@ -156,44 +206,48 @@
 
     @pl.when(jnp.logical_not(gathers))
     def _():
-        pl.semaphore_wait(barrier, n_gather + len(halo_steps))
+        pl.semaphore_wait(barrier, n_gather + others + len(halo_steps))
+        send_early()
         for to_z in range(planes):
             for to_core in range(2):
                 send_row(column(to_z, to_core))
 
     recent = jnp.maximum(count_here - 2, 0)
     last_row = jnp.maximum(length_here - 1, 0)
+    top, low = 2 * height, 2 * height + frames + 2
     for k in range(2):
-        tail[k] = block[recent + k]
-        rising[k] = tail[k, last_row]
-        sinking[k] = tail[k, 0]
+        for r in range(height):
+            leaving[k * height + r] = block[recent + k, r]
+        leaving[top + k] = block[recent + k, last_row]
+        leaving[low + k] = block[recent + k, 0]
     for k in range(frames):
-        rising[2 + k] = block[k, last_row]
-        sinking[2 + k] = block[k, 0]
-    here, before = pl.ds(2, frames), pl.ds(0, 2)
-    halos = [
-        (rising.at[here], upper.at[here], (0, 1)),
-        (sinking.at[here], lower.at[here], (0, -1)),
-        (rising.at[before], upper.at[before], (1, 1)),
-        (sinking.at[before], lower.at[before], (1, -1)),
-        (tail, prior, (1, 0)),
-    ]
-    halos = [
+        leaving[top + 2 + k] = block[k, last_row]
+        leaving[low + 2 + k] = block[k, 0]
+    for start, size, step in (
+        (top + 2, frames, (0, 1)), (low + 2, frames, (0, -1)),
+        (top, 2, (1, 1)), (low, 2, (1, -1)), (0, top, (1, 0)),
+    ):
+        part = pl.ds(start, size)
         pltpu.make_async_remote_copy(
-            src_ref=source, dst_ref=target, send_sem=halo_send.at[i], recv_sem=halo_sems.at[i],
+            src_ref=leaving.at[part], dst_ref=halo.at[part], send_sem=halo_send, recv_sem=halo_sem,
             device_id=beside(*step), device_id_type=MESH,
-        )
-        for i, (source, target, step) in enumerate(halos)
-    ]
-    for halo in halos:
-        halo.start()
-    widen = group_matrix(channels, 0, True) + group_matrix(channels, GROUPS, True)
+        ).start()
+    for source, target in ((gain_in, gain), (shift_in, shift), (bias_in, bias)):
+        small = pltpu.make_async_copy(source, target, load_sem)
+        small.start()
+        small.wait()
+    widen = group_matrix(channels, 2 * GROUPS, True) + group_matrix(channels, 3 * GROUPS, True)
+
+    def settle():
+        fetch.wait()
+        pltpu.make_async_copy(leaving, leaving, halo_send).wait()
+        pltpu.make_async_copy(halo, halo, halo_sem).wait()
 
     def answers():
         base = jnp.where(z == 1, planes + half, planes)
         return [
             pltpu.make_async_remote_copy(
-                src_ref=result.at[0], dst_ref=result.at[0], send_sem=result_send.at[k],
+                src_ref=result.at[0], dst_ref=result.at[0], send_sem=result_send,
                 recv_sem=result_sem, device_id=column(base + k // 2, k % 2), device_id_type=MESH,
             )
             for k in range(4)
@@ -205,28 +259,42 @@
         pltpu.make_async_copy(sent, sent, row_send).wait()
         arrived = first.at[pl.ds(0, n_column - 1)]
         pltpu.make_async_copy(arrived, arrived, first_sem).wait()
-        second[0] = as_row(*merge([first[i] for i in range(n_column)]))
-        copies = [
-            pltpu.make_async_remote_copy(
-                src_ref=second.at[0], dst_ref=second.at[1 + i], send_sem=second_send,
-                recv_sem=second_sem, device_id=far(*step), device_id_type=MESH,
-            )
-            for i, step in enumerate(far_steps)
-        ]
-        for copy in copies:
-            copy.start()
-        for copy in ahead:
-            copy.wait()
-        for halo in halos:
-            halo.wait()
-        sent = second.at[pl.ds(1, len(far_steps))]
-        pltpu.make_async_copy(sent, sent, second_send).wait()
-        pltpu.make_async_copy(sent, sent, second_sem).wait()
-        totals, spread, entries = merge([second[i] for i in range(1 + len(far_steps))])
-        mean = totals / entries
-        scale = lax.rsqrt(spread / entries + EPSILON)
-        lane = lax.broadcasted_iota(jnp.int32, mean.shape, 1)
-        result[0] = jnp.where(lane < GROUPS, mean, pltpu.roll(scale, GROUPS, 1))
+        totals, mean, spread, entries = merge(first[...].reshape(n_column, LANES))
+        second[0] = as_row(totals, mean, spread)
+
+        def for_peers(act):
+            for i, (dx, dy) in enumerate(far_steps):
+                @pl.when(jnp.logical_not(is_early((x + dx) % size_x, (y + dy) % size_y, z)))
+                def _():
+                    act(pltpu.make_async_remote_copy(
+                        src_ref=second.at[0], dst_ref=second.at[1 + i], send_sem=second_send,
+                        recv_sem=second_sem, device_id=far(dx, dy), device_id_type=MESH,
+                    ))
+
+        for_peers(lambda copy: copy.start())
+        settle()
+        for plane in range(planes):
+            spared = sum(1 for device in direct if device[0] % 2 and device[1] % size_z == plane)
+            for mine in range(2 if spared else 1):
+                @pl.when((z == plane) & (early if mine else jnp.logical_not(early)))
+                def _():
+                    sent = second.at[pl.ds(0, len(far_steps) - spared + mine)]
+                    pltpu.make_async_copy(sent, sent, second_send).wait()
+
+        @pl.when(early)
+        def _():
+            sent_early(len(direct) - 1)
+            table[rank] = row[0]
+            arrived = table.at[pl.ds(0, n_devices - 1)]
+            pltpu.make_async_copy(arrived, arrived, direct_sem).wait()
+            result[0] = as_result(*merge(table[...].reshape(n_devices, LANES)))
+
+        @pl.when(jnp.logical_not(early))
+        def _():
+            sent_early(len(direct))
+            arrived = second.at[pl.ds(1, len(far_steps))]
+            pltpu.make_async_copy(arrived, arrived, second_sem).wait()
+            result[0] = as_result(*merge(second[...].reshape(1 + len(far_steps), LANES)))
 
         @pl.when(serves)
         def _():
@@ -237,31 +305,30 @@
     def _():
         sent = first.at[pl.ds(0, n_gather)]
         pltpu.make_async_copy(sent, sent, row_send).wait()
-        for copy in ahead:
-            copy.wait()
-        for halo in halos:
-            halo.wait()
+        sent_early(len(direct))
+        settle()
         pltpu.make_async_copy(result.at[0], result.at[0], result_sem).wait()
 
     both = jnp.broadcast_to(result[0], (8, LANES))
     lane = lax.broadcasted_iota(jnp.int32, both.shape, 1)
     sub = lax.broadcasted_iota(jnp.int32, both.shape, 0)
-    stats[...] = exact_dot(jnp.where(lane // GROUPS == sub, both, 0.0), widen)
+    stats[...] = exact_dot(jnp.where(lane // GROUPS == sub + 2, both, 0.0), widen)
 
     @pl.when(serves)
     def _():
-        for answer in answers():
-            answer.wait_send()
+        sent = first.at[pl.ds(0, 4)]
+        pltpu.make_async_copy(sent, sent, result_send).wait()
 
 
 def convolve_kernel(
-    n_tile, features, prior, upper, lower, stats, weights, gain, shift, bias, counts, lengths,
+    n_tile, features, halo, stats, weights, gain, shift, bias, counts, lengths,
     out_hbm,
-    out, stacked, q0, q1, q2, woven, hidden, out_sems,
+    out, stacked, q0, q1, q2, woven, hidden, out_sem,
 ):
     frames, height, width, channels = features.shape
     slots, run, depth = height + 2, frames * width, 3 * channels
     products = (q0, q1, q2)
+    top, low = 2 * height, 2 * height + frames + 2
     tm, tile = lax.axis_index("tm"), lax.axis_index("tile")
     count_here = counts[0]
     length_here = lengths[0]
@@ -275,15 +342,15 @@
         blank = (slot == 0) & (tile == 0) | is_lower & (tile == n_tile - 1)
         frame = jnp.where(tm == 0, 2, k) if k < 2 else k
         if slot == 0:
-            v = upper[frame]
+            v = halo[top + frame]
         elif slot == slots - 1:
-            v = lower[frame]
+            v = halo[low + frame]
         else:
-            v = prior[k, slot - 1] if k < 2 else features[k - 2, slot - 1]
+            v = halo[k * height + slot - 1] if k < 2 else features[k - 2, slot - 1]
             if k < 2:
                 v = jnp.where(tm == 0, features[0, slot - 1], v)
             if slot > 1:
-                v = jnp.where(is_lower, lower[frame], v)
+                v = jnp.where(is_lower, halo[low + frame], v)
         v = v.astype(jnp.float32)
         v = (v - mean) * scale + offset
         v = v / (1.0 + jnp.exp(-v))
@@ -319,7 +386,7 @@
             out[t, 2 * r + s, :, lanes] = woven[slab, i].astype(jnp.bfloat16)
 
     def leave(row):
-        return pltpu.make_async_copy(out.at[:, row], out_hbm.at[:, row], out_sems.at[row])
+        return pltpu.make_async_copy(out.at[:, row], out_hbm.at[:, row], out_sem)
 
     def preparing(slot):
         work = [functools.partial(normalise, slot, k) for k in range(frames + 2)]
@@ -350,8 +417,7 @@
             done = upto
     for piece in finishing(height - 1, 1):
         piece()
-    for row in range(2 * height):
-        leave(row).wait()
+    pltpu.make_async_copy(out, out_hbm, out_sem).wait()
 
 
 def body(dims, features, frame_counts, row_lengths, norm_gain, norm_shift, conv_weight, conv_bias):
@@ -363,13 +429,11 @@
     in_vmem = pl.BlockSpec(memory_space=pltpu.VMEM)
     in_smem = pl.BlockSpec(memory_space=pltpu.SMEM)
     bf16, f32 = jnp.bfloat16, jnp.float32
-    halo = (frames + 2, width, channels)
+    halo = (2 * height + 2 * (frames + 2), width, channels)
     ready = pl.pallas_call(
         functools.partial(exchange_kernel, dims),
         out_shape=(
             pltpu.VMEM(features.shape, bf16),
-            pltpu.VMEM((2, height, width, channels), bf16),
-            pltpu.VMEM(halo, bf16),
             pltpu.VMEM(halo, bf16),
             pltpu.VMEM((8, channels), f32),
             pltpu.VMEM(conv_weight.shape, bf16),
@@ -378,25 +442,16 @@
             pltpu.VMEM((1, made), f32),
         ),
         in_specs=[anywhere] * 5 + [in_smem] * 2,
-        out_specs=(in_vmem,) * 9,
+        out_specs=(in_vmem,) * 7,
         scratch_shapes=[
-            pltpu.VMEM((2, height, width, channels), bf16),
-            pltpu.VMEM(halo, bf16),
             pltpu.VMEM(halo, bf16),
             pltpu.VMEM((1, 1, LANES), f32),
             pltpu.VMEM((size_z * 2, 1, LANES), f32),
             pltpu.VMEM((size_x * size_y, 1, LANES), f32),
+            pltpu.VMEM((n_tm * n_tile, 1, LANES), f32),
             pltpu.VMEM((1, 1, LANES), f32),
-            pltpu.SemaphoreType.DMA((5,)),
-            pltpu.SemaphoreType.DMA,
-            pltpu.SemaphoreType.DMA,
-            pltpu.SemaphoreType.DMA,
-            pltpu.SemaphoreType.DMA,
-            pltpu.SemaphoreType.DMA((4,)),
-            pltpu.SemaphoreType.DMA,
-            pltpu.SemaphoreType.DMA((5,)),
-            pltpu.SemaphoreType.DMA((5,)),
-        ],
+        ]
+        + [pltpu.SemaphoreType.DMA] * 12,
         compiler_params=pltpu.CompilerParams(
             collective_id=0, has_side_effects=True, vmem_limit_bytes=EXCHANGE_VMEM
         ),
@@ -408,7 +463,7 @@
     return pl.pallas_call(
         functools.partial(convolve_kernel, n_tile),
         out_shape=jax.ShapeDtypeStruct((frames, 2 * height, 2 * width, made), bf16),
-        in_specs=[in_vmem] * 9 + [in_smem] * 2,
+        in_specs=[in_vmem] * 7 + [in_smem] * 2,
         out_specs=anywhere,
         scratch_shapes=[
             pltpu.VMEM((frames, 2 * height, 2 * width, made), bf16),
@@ -418,7 +473,7 @@
             pltpu.VMEM((3, height + 2, run, made), f32),
             pltpu.VMEM((2 * height * frames, made // LANES, 2 * width, LANES), f32),
             pltpu.VMEM((2, (frames + 2) * width, channels), f32),
-            pltpu.SemaphoreType.DMA((2 * height,)),
+            pltpu.SemaphoreType.DMA,
         ],
         compiler_params=pltpu.CompilerParams(vmem_limit_bytes=CONVOLVE_VMEM),
         name="convolve",

time: 25.3 us -> 24.4 us (0.964)
  Pallas kernels: 23.9 us -> 23 us
    pallas_call x1, Pallas kernels: 18.7 us -> 17.8 us  [body(): pl.pallas_call(functools.partial(exchange_kernel, dims), out_shape=(pltpu...]
where the time goes in v4:
time: 24.4 us; the launch traced here: 24.3 us
  Pallas kernels  23 us (94%)
  between operations  1.31 us (5%)
    pallas_call x1, Pallas kernels, body(): pl.pallas_call(functools.partial(exchange_kernel, dims), out_shape=(pltpu...  17.8 us
    pallas_call x1, Pallas kernels, body(): pl.pallas_call(functools.partial(convolve_kernel, n_tile), out_shape=jax....  5.19 us

profile of v4, /device:TPU:1, one launch (start us, length us, event | category | flops | bytes accessed | tf_op | source)
XLA Modules:
  0.0 24.3 jit_solution(3200012186819064024)
XLA Ops:
  1.3 17.8 %exchange.1 = (bf16[6,3,24,512]{3,2,1,0:T(8,128)(2,1)S(1)}, bf16[22,24,512]{2,1,0:T(8,128)(2,1)S(1)}, f32[8,512]{1,0:T(8,128)S(1)}, bf16[3,3,3,512,256]{4,3,2,1,...) custom-call(bf16[6,3,24,512]{3,2,1,0:T(8,128)(2,1)} %features.1, ...), custom_call_target="tpu_custom_call" | custom-call | tf_op jit(solution)/shard_map/exchange/pallas_call | solution.py:433
  19.1 5.2 %convolve.1 = bf16[6,6,48,256]{3,2,1,0:T(8,128)(2,1)} custom-call(bf16[6,3,24,512]{3,2,1,0:T(8,128)(2,1)S(1)} %get-tuple-element.12.features, bf16[22,24,512]{2,1,0:T(8,128)(2,1)S(1)} %get-tuple-element.13.halo, f32[8,512]{1,0:T(8,128)S(1)} %get-tuple-element.14.stats, bf16[3,3,3,512,256]{4,3,2,1,0:T(8,128)(2,1)S(1)} %get-tuple-element.15.weights, ...), custom_call_target="tpu_custom_call" | custom-call | tf_op jit(solution)/shard_map/convolve/pallas_call | solution.py:463

commit v5 on v4

--- a/solution.py
+++ b/solution.py
@@ -100,7 +100,16 @@
     n_devices = n_tm * n_tile
 
     far_steps = [(dx, dy) for dx in range(size_x) for dy in range(size_y)][1:]
-    halo_steps = [(a, b) for a in (-1, 0, 1) for b in (-1, 0, 1) if (a, b) != (0, 0)]
+    top, low = 2 * height, 2 * height + frames + 2
+    parts = [
+        (top + 2, frames, (0, 1)), (low + 2, frames, (0, -1)),
+        (top, 2, (1, 1)), (low, 2, (1, -1)), (0, top, (1, 0)),
+    ]
+
+    def inside(dt, dr):
+        return (tm + dt >= 0) & (tm + dt < n_tm) & (tile + dr >= 0) & (tile + dr < n_tile)
+
+    halo_known = sum(jnp.where(inside(*step), 1, 0) for _, _, step in parts)
     n_column, n_gather = 2 * size_z, 2 * planes
 
     load = pltpu.make_async_copy(features, block, load_sem)
@@ -111,8 +120,10 @@
     def greet(device):
         pl.semaphore_signal(barrier, inc=1, device_id=device, device_id_type=MESH)
 
-    for step in halo_steps:
-        greet(beside(*step))
+    for _, _, (dt, dr) in parts:
+        @pl.when(inside(-dt, -dr))
+        def _():
+            greet(beside(-dt, -dr))
 
     @pl.when(gathers)
     def _():
@@ -195,7 +206,7 @@
 
     @pl.when(gathers)
     def _():
-        known = n_gather - 1 + len(far_steps) + len(halo_steps)
+        known = n_gather - 1 + len(far_steps) + halo_known
         pl.semaphore_wait(barrier, known + others + jnp.where(serves, 4, 0))
         send_early()
         first[own] = row[0]
@@ -206,7 +217,7 @@
 
     @pl.when(jnp.logical_not(gathers))
     def _():
-        pl.semaphore_wait(barrier, n_gather + others + len(halo_steps))
+        pl.semaphore_wait(barrier, n_gather + others + halo_known)
         send_early()
         for to_z in range(planes):
             for to_core in range(2):
@@ -214,7 +225,6 @@
 
     recent = jnp.maximum(count_here - 2, 0)
     last_row = jnp.maximum(length_here - 1, 0)
-    top, low = 2 * height, 2 * height + frames + 2
     for k in range(2):
         for r in range(height):
             leaving[k * height + r] = block[recent + k, r]
@@ -223,15 +233,19 @@
     for k in range(frames):
         leaving[top + 2 + k] = block[k, last_row]
         leaving[low + 2 + k] = block[k, 0]
-    for start, size, step in (
-        (top + 2, frames, (0, 1)), (low + 2, frames, (0, -1)),
-        (top, 2, (1, 1)), (low, 2, (1, -1)), (0, top, (1, 0)),
-    ):
-        part = pl.ds(start, size)
+    halos = [
         pltpu.make_async_remote_copy(
-            src_ref=leaving.at[part], dst_ref=halo.at[part], send_sem=halo_send, recv_sem=halo_sem,
+            src_ref=leaving.at[pl.ds(start, size)], dst_ref=halo.at[pl.ds(start, size)],
+            send_sem=halo_send.at[i], recv_sem=halo_sem.at[i],
             device_id=beside(*step), device_id_type=MESH,
-        ).start()
+        )
+        for i, (start, size, step) in enumerate(parts)
+    ]
+    for copy, (_, _, step) in zip(halos, parts):
+        @pl.when(inside(*step))
+        def _():
+            copy.start()
+
     for source, target in ((gain_in, gain), (shift_in, shift), (bias_in, bias)):
         small = pltpu.make_async_copy(source, target, load_sem)
         small.start()
@@ -240,8 +254,14 @@
 
     def settle():
         fetch.wait()
-        pltpu.make_async_copy(leaving, leaving, halo_send).wait()
-        pltpu.make_async_copy(halo, halo, halo_sem).wait()
+        for copy, (_, _, (dt, dr)) in zip(halos, parts):
+            @pl.when(inside(dt, dr))
+            def _():
+                copy.wait_send()
+
+            @pl.when(inside(-dt, -dr))
+            def _():
+                copy.wait_recv()
 
     def answers():
         base = jnp.where(z == 1, planes + half, planes)
@@ -451,7 +471,8 @@
             pltpu.VMEM((n_tm * n_tile, 1, LANES), f32),
             pltpu.VMEM((1, 1, LANES), f32),
         ]
-        + [pltpu.SemaphoreType.DMA] * 12,
+        + [pltpu.SemaphoreType.DMA] * 10
+        + [pltpu.SemaphoreType.DMA((5,))] * 2,
         compiler_params=pltpu.CompilerParams(
             collective_id=0, has_side_effects=True, vmem_limit_bytes=EXCHANGE_VMEM
         ),

time: 24.4 us -> 24.1 us (0.988)
  Pallas kernels: 23 us -> 22.7 us
    pallas_call x1, Pallas kernels: 17.8 us -> 17.5 us  [body(): pl.pallas_call(functools.partial(exchange_kernel, dims), out_shape=(pltpu...]
where the time goes in v5:
time: 24.1 us; the launch traced here: 24 us
  Pallas kernels  22.7 us (94%)
  between operations  1.31 us (5%)
    pallas_call x1, Pallas kernels, body(): pl.pallas_call(functools.partial(exchange_kernel, dims), out_shape=(pltpu...  17.5 us
    pallas_call x1, Pallas kernels, body(): pl.pallas_call(functools.partial(convolve_kernel, n_tile), out_shape=jax....  5.19 us

profile of v5, /device:TPU:1, one launch (start us, length us, event | category | flops | bytes accessed | tf_op | source)
XLA Modules:
  0.0 24.0 jit_solution(8534596189613241584)
XLA Ops:
  1.3 17.5 %exchange.1 = (bf16[6,3,24,512]{3,2,1,0:T(8,128)(2,1)S(1)}, bf16[22,24,512]{2,1,0:T(8,128)(2,1)S(1)}, f32[8,512]{1,0:T(8,128)S(1)}, bf16[3,3,3,512,256]{4,3,2,1,...) custom-call(bf16[6,3,24,512]{3,2,1,0:T(8,128)(2,1)} %features.1, ...), custom_call_target="tpu_custom_call" | custom-call | tf_op jit(solution)/shard_map/exchange/pallas_call | solution.py:453
  18.8 5.2 %convolve.1 = bf16[6,6,48,256]{3,2,1,0:T(8,128)(2,1)} custom-call(bf16[6,3,24,512]{3,2,1,0:T(8,128)(2,1)S(1)} %get-tuple-element.12.features, bf16[22,24,512]{2,1,0:T(8,128)(2,1)S(1)} %get-tuple-element.13.halo, f32[8,512]{1,0:T(8,128)S(1)} %get-tuple-element.14.stats, bf16[3,3,3,512,256]{4,3,2,1,0:T(8,128)(2,1)S(1)} %get-tuple-element.15.weights, ...), custom_call_target="tpu_custom_call" | custom-call | tf_op jit(solution)/shard_map/convolve/pallas_call | solution.py:484
